TPU v7x, 256 devices: a whole 4x4x8 slice. The times are simulated.
256 devices in a mesh: seq: 64 (over y, z, core), tp: 4 (over x).
Axes of the slice: x: 4, y: 4, z: 8, core: 2. Of those that a mesh axis runs over, the one named last changes fastest.
Arguments:
- queries: bfloat16 [98304, 2048], P('seq', 'tp'), may hold values from -160 to 160
- cotangent: bfloat16 [98304, 2048], P('seq', 'tp'), may hold values from -6 to 6
- owner_map: int32 [1536, 1], P('seq'), may hold values from 0 to 63; in each aligned block of 24 rows (0 to 23, 24 to 47, ...) at most 2 rows name the same one
- neighbour_ids: int32 [1536, 2], P('seq'), may hold values from 0 to 1
- database: bfloat16 [128, 128, 1536], P('seq', None, 'tp'), may hold values from -6 to 6
- norm_gain: float32 [1536], P('tp'), may hold values from 0.5 to 2
- key_weight: bfloat16 [1536, 2048], P(None, 'tp'), may hold values from -0.15625 to 0.15625
- value_weight: bfloat16 [1536, 2048], P(None, 'tp'), may hold values from -0.15625 to 0.15625
Outputs:
- attended: bfloat16 [98304, 2048], P('seq', 'tp')
- grad_key_weight: float32 [1536, 2048], P('seq', 'tp')
Inputs may be any that keep to these rules, and one draw needn't show every extreme that they name: `owner_map`: in each aligned block of 24 spans (the spans of one index of seq) no owner is named more than 2 times, a bound that some block reaches.
All inputs are finite; a program needn't handle non-finite values.
Results may differ from a plain program's by a relative error of at most 0.01.
The roundings to bfloat16 on the way count: a program that leaves them out, or rounds other values in their place, can miss the bound.
Values may be sent and summed in bfloat16 or wider, within the bound.
No kernel may reach another device: no remote copies, remote signals or barrier semaphores. Data moves between devices by JAX's collectives and lax.ppermute only.
A program may use at most 128 MiB of HBM per device.

v0:
```python
import functools
import math

import jax
import jax.numpy as jnp
from jax import lax
from jax.experimental import pallas as pl
from jax.experimental.pallas import tpu as pltpu
from jax.sharding import PartitionSpec as P

D_HEAD = 128
SPAN = 64
NLEN = 128
N_Y, N_Z = 4, 8
CHIPS = N_Y * N_Z
TOGETHER = 4
epsilon = 1e-06


def seq_of(y, z, core):
    return ((y % N_Y) * N_Z + z % N_Z) * 2 + core


PAIR = [(i, i ^ 1) for i in range(2 * CHIPS)]
Z_GROUPS = [[seq_of(y, z, c) for z in range(N_Z)] for y in range(N_Y) for c in range(2)]
Y_GROUPS = [[seq_of(y, z, c) for y in range(N_Y)] for z in range(N_Z) for c in range(2)]
CELLS = [(y, z, c) for y in range(N_Y) for z in range(N_Z) for c in range(2)]
NT = (((1,), (1,)), ((), ()))
TN = (((0,), (0,)), ((), ()))


def swap(x):
    with jax.named_scope("swap"):
        return lax.ppermute(x, "seq", PAIR)


def from_y(x, step):
    with jax.named_scope("y"):
        return lax.ppermute(x, "seq", [(seq_of(y + step, z, c), seq_of(y, z, c)) for y, z, c in CELLS])


def from_z(x, step):
    with jax.named_scope("z"):
        return lax.ppermute(x, "seq", [(seq_of(y, z + step, c), seq_of(y, z, c)) for y, z, c in CELLS])


def add(x, *others):
    total = x.astype(jnp.float32)
    for other in others:
        total = total + other.astype(jnp.float32)
    return total.astype(jnp.bfloat16)


def after(values, done):
    return lax.optimization_barrier((values, done))[0]


def halves(x):
    middle = x.shape[0] // 2
    return x[:middle], x[middle:]


def ring_near(x, fetch, size):
    up, down, parts = x, x, [x]
    for hop in range(1, size // 2):
        with jax.named_scope(f"gather_{hop}"):
            up, down = fetch(up, 1), fetch(down, -1)
        parts += [up, down]
    return parts


def ring_far(parts, fetch):
    with jax.named_scope("gather_far"):
        return [fetch(halves(parts[-2])[0], 1), fetch(halves(parts[-1])[1], -1)]


def ring_gather(x, fetch, size):
    parts = ring_near(x, fetch, size)
    return parts + ring_far(parts, fetch)


def join(parts):
    return jnp.stack(parts[:-2] + [jnp.concatenate(parts[-2:])])


def ring_scatter(parts, fetch, size):
    with jax.named_scope("scatter_far"):
        first, second = fetch(parts[-2], -1), fetch(parts[-1], 1)
    plus, minus = parts[size - 3], parts[size - 2]
    plus = jnp.concatenate([add(halves(plus)[0], first), halves(plus)[1]])
    minus = jnp.concatenate([halves(minus)[0], add(halves(minus)[1], second)])
    for hop in range(size // 2 - 2, 0, -1):
        with jax.named_scope(f"scatter_{hop + 1}"):
            plus, minus = (
                add(parts[2 * hop - 1], fetch(plus, -1)),
                add(parts[2 * hop], fetch(minus, 1)),
            )
    with jax.named_scope("scatter_1"):
        return add(parts[0], fetch(plus, -1), fetch(minus, 1))


def ring_place(offset, size):
    offset = offset % size
    place = jnp.where(offset < size // 2, 2 * offset - 1, 2 * (size - offset))
    place = jnp.where(offset == size // 2, size - 1, place)
    return jnp.where(offset == 0, 0, place)


def work_list(place, member, first, last):
    spans = place.shape[0]
    chosen = member & (place >= first) & (place < last)
    order = jnp.arange(spans)
    before = order[None, :] < order[:, None]
    rank = jnp.sum((before & chosen[None, :]).astype(jnp.int32), axis=1)
    at = chosen[None, :] & (rank[None, :] == order[:, None])
    listed = jnp.sum(jnp.where(at, order[None, :], 0), axis=1)
    block = jnp.sum(jnp.where(at, place[None, :] - first, 0), axis=1)
    number = jnp.sum(chosen.astype(jnp.int32)).reshape(1)
    return number, listed.astype(jnp.int32), block.astype(jnp.int32)


def attention_kernel(heads, sizes, earlier, number, listed, block, ids, *refs):
    parts = len(sizes)
    q_ref, cot_ref = refs[:2]
    sources = refs[2 : 2 + parts]
    refs = refs[2 + parts :]
    if earlier:
        before_ref, refs = refs[0], refs[1:]
    att_ref, refs = refs[0], refs[1:]
    grad_refs = refs[:parts]
    kv, acc, semaphores = refs[parts:]
    inv_root = 1.0 / math.sqrt(D_HEAD)
    dot = functools.partial(lax.dot_general, preferred_element_type=jnp.float32)

    copies, start = [], 0
    for i, size in enumerate(sizes):
        copies.append(
            pltpu.make_async_copy(sources[i], kv.at[pl.ds(start, size)], semaphores.at[i])
        )
        copies[-1].start()
        start += size
    acc[...] = jnp.zeros_like(acc)
    if earlier:
        att_ref[...] = before_ref[...]
    for copy in copies:
        copy.wait()

    first_half = lax.broadcasted_iota(jnp.int32, (1, 2 * NLEN), 1) < NLEN
    amount = number[0]
    key_cols = [slice(h * D_HEAD, (h + 1) * D_HEAD) for h in range(heads)]
    value_cols = [slice((heads + h) * D_HEAD, (heads + h + 1) * D_HEAD) for h in range(heads)]

    def step(i, carry):
        items = []
        for u in range(TOGETHER):
            k = i * TOGETHER + u
            at = jnp.minimum(k, amount - 1)
            span, place = listed[at], block[at]
            rows = pl.ds(pl.multiple_of(span * SPAN, SPAN), SPAN)
            one, two = ids[2 * span], ids[2 * span + 1]
            low = jnp.where((one == 0) | (two == 0), 0.0, -1e30)
            high = jnp.where((one == 1) | (two == 1), 0.0, -1e30)
            bias = jnp.where(first_half, low, high)
            scale = jnp.where(k < amount, inv_root, 0.0)
            items += [(rows, place, bias, scale, h) for h in range(heads)]
        q = [q_ref[rows, key_cols[h]] for rows, _, _, _, h in items]
        scores = [
            dot(x, kv[place, :, key_cols[h]], NT) * (inv_root * math.log2(math.e)) + bias
            for x, (_, place, bias, _, h) in zip(q, items)
        ]
        grad_probs = [
            dot(cot_ref[rows, key_cols[h]], kv[place, :, value_cols[h]], NT)
            for rows, place, _, _, h in items
        ]
        highest = [jnp.max(s, axis=1, keepdims=True) for s in scores]
        weights = [jnp.exp2(s - m) for s, m in zip(scores, highest)]
        sums = [jnp.sum(w, axis=1, keepdims=True) for w in weights]
        probs = [w * (1.0 / s) for w, s in zip(weights, sums)]
        deltas = [jnp.sum(p * g, axis=1, keepdims=True) for p, g in zip(probs, grad_probs)]
        grad_scores = [
            (p * (g - d) * item[3]).astype(jnp.bfloat16)
            for p, g, d, item in zip(probs, grad_probs, deltas, items)
        ]
        for p, (rows, place, _, _, h) in zip(probs, items):
            att = jnp.dot(
                p.astype(jnp.bfloat16),
                kv[place, :, value_cols[h]],
                preferred_element_type=jnp.float32,
            )
            att_ref[rows, key_cols[h]] = att.astype(jnp.bfloat16)
        for x, g, (_, place, _, _, h) in zip(q, grad_scores, items):
            acc[place, key_cols[h]] += dot(x, g, TN)
        return carry

    lax.fori_loop(0, (amount + TOGETHER - 1) // TOGETHER, step, 0)

    start = 0
    for ref, size in zip(grad_refs, sizes):

        def round_block(b, carry, ref=ref, start=start):
            ref[b] = acc[start + b].astype(jnp.bfloat16)
            return carry

        lax.fori_loop(0, size, round_block, 0)
        start += size


def attend(work, ids, q, cot, column, parts, earlier=None):
    seen, width = parts[0].shape[1], parts[0].shape[2] // 2
    heads, tokens = width // D_HEAD, q.shape[0]
    sizes = [part.shape[0] for part in parts]
    whole = pl.BlockSpec((tokens, width), lambda i, *_: (0, 0))
    chunk = pl.BlockSpec((tokens, width), lambda i, *_: (0, column))
    before = [] if earlier is None else [earlier]
    out = pl.pallas_call(
        functools.partial(attention_kernel, heads, sizes, bool(before)),
        grid_spec=pltpu.PrefetchScalarGridSpec(
            num_scalar_prefetch=4,
            grid=(1,),
            in_specs=[chunk, chunk]
            + [pl.BlockSpec(memory_space=pl.ANY)] * len(parts)
            + [whole] * len(before),
            out_specs=[whole]
            + [pl.BlockSpec((size, width, seen), lambda i, *_: (0, 0, 0)) for size in sizes],
            scratch_shapes=[
                pltpu.VMEM((sum(sizes), seen, 2 * width), jnp.bfloat16),
                pltpu.VMEM((sum(sizes), width, seen), jnp.float32),
                pltpu.SemaphoreType.DMA((len(sizes),)),
            ],
        ),
        out_shape=[jax.ShapeDtypeStruct((tokens, width), jnp.bfloat16)]
        + [jax.ShapeDtypeStruct((size, width, seen), jnp.bfloat16) for size in sizes],
        compiler_params=pltpu.CompilerParams(vmem_limit_bytes=48 * 1024 * 1024),
        cost_estimate=pl.CostEstimate(
            flops=tokens * seen * width * 4,
            bytes_accessed=sum(sizes) * seen * width * 6 + tokens * width * 6,
            transcendentals=tokens * seen * heads,
        ),
    )(*work, ids, q, cot, *parts, *before)
    return out[0], list(out[1:])


def normed_store(database, norm_gain):
    rows = database.reshape(-1, database.shape[2])
    stored = rows.shape[0]
    top = lax.reduce_precision(norm_gain, 8, 7)
    middle = lax.reduce_precision(norm_gain - top, 8, 7)
    bottom = norm_gain - top - middle
    gains = jnp.stack([top, middle, bottom]).astype(jnp.bfloat16)
    packed = jnp.concatenate([rows, jnp.pad(gains, ((0, 13), (0, 0)))], axis=0)
    whole = lax.all_gather(packed, "tp", axis=1, tiled=True).astype(jnp.float32)
    floats = whole[:stored]
    gain = whole[stored] + whole[stored + 1] + whole[stored + 2]
    mean = jnp.sum(floats * floats, axis=1, keepdims=True) / floats.shape[1]
    return (floats * lax.rsqrt(mean + epsilon) * gain[None, :]).astype(jnp.bfloat16)


def core_rows(x, core):
    return lax.dynamic_index_in_dim(x.reshape(x.shape[0], CHIPS, 2, -1), core, 2, False)


def scatter_gradient(total, rows):
    width = total.shape[1]
    for groups in (Y_GROUPS, Z_GROUPS):
        size = len(groups[0])
        total = total.astype(jnp.bfloat16).reshape(size, -1, rows, width)
        total = lax.all_to_all(total, "seq", 0, 0, axis_index_groups=groups, tiled=True)
        total = jnp.sum(total.astype(jnp.float32), axis=0)
    return total.reshape(rows, width)


def per_device(
    queries, cotangent, owner_map, neighbour_ids, database, norm_gain, key_weight, value_weight
):
    core = lax.axis_index("seq") % 2
    tokens, local_width = queries.shape
    width = local_width // 2

    meta = jnp.concatenate([owner_map, neighbour_ids], axis=1)
    meta = jnp.concatenate([meta, swap(meta)], axis=0)
    q = jnp.concatenate([queries, swap(queries)], axis=0)
    cot = jnp.concatenate([cotangent, swap(cotangent)], axis=0)
    owners, ids = meta[:, 0], meta[:, 1:].reshape(-1)
    chip = lax.axis_index("seq") // 2
    member = owners % 2 == core
    y_place = ring_place(owners // (2 * N_Z) - chip // N_Z, N_Y)
    z_place = ring_place(owners // 2 - chip, N_Z)

    normed = normed_store(database, norm_gain)
    key_rows = jnp.dot(normed, key_weight, preferred_element_type=jnp.float32).astype(jnp.bfloat16)
    value_rows = jnp.dot(normed, value_weight, preferred_element_type=jnp.float32).astype(
        jnp.bfloat16
    )

    chip_normed = [core_rows(normed, core), swap(core_rows(normed, 1 - core))]
    chip_normed = jnp.concatenate(chip_normed, axis=0).reshape(2 * normed.shape[0], -1)

    kv = [
        jnp.concatenate([r[:, i * width : (i + 1) * width] for r in (key_rows, value_rows)], axis=1)
        for i in range(2)
    ]

    place_one = y_place * N_Z + z_place
    place_two = z_place * N_Y + y_place
    work_one = functools.partial(work_list, place_one, member)
    work_two = functools.partial(work_list, place_two, member)

    with jax.named_scope("one"):
        line_one = join(ring_gather(kv[0], from_z, N_Z))
        one = ring_near(line_one, from_y, N_Y)
    with jax.named_scope("two"):
        line_two = join(ring_gather(kv[1], from_y, N_Y))
        two = ring_near(line_two, from_z, N_Z)
    with jax.named_scope("two_near"):
        att_two, grads_two = attend(work_two(0, 5 * N_Y), ids, q, cot, 1, two[:5])
    with jax.named_scope("two"):
        two[-2:] = after(two[-2:], att_two)
        two += ring_far(two, from_z)
    with jax.named_scope("one"):
        one[-2:] = after(one[-2:], att_two)
        one += ring_far(one, from_y)
    with jax.named_scope("one_near"):
        att_one, grads_one = attend(work_one(0, 3 * N_Z), ids, q, cot, 0, one[:3])
    with jax.named_scope("two_far"):
        att_two, more = attend(
            work_two(5 * N_Y, CHIPS), ids, q, cot, 1, two[5:], after(att_two, att_one)
        )
        grads_two += more
    with jax.named_scope("one_far"):
        att_one, more = attend(
            work_one(3 * N_Z, CHIPS), ids, q, cot, 0, one[3:], after(att_one, att_two)
        )
        grads_one += more

    with jax.named_scope("two"):
        sums = ring_scatter(grads_two, from_z, N_Z)
        grad_two = ring_scatter([*sums[:-1], *halves(sums[-1])], from_y, N_Y)
    with jax.named_scope("one"):
        sums = ring_scatter(grads_one, from_y, N_Y)
        grad_one = ring_scatter([*sums[:-1], *halves(sums[-1])], from_z, N_Z)

    here = owner_map % 2 == core
    here = jnp.broadcast_to(here, (here.shape[0], SPAN)).reshape(tokens, 1)
    attended = [jnp.where(here, att[:tokens], swap(att[tokens:])) for att in (att_one, att_two)]
    grad_keys = jnp.concatenate([grad_one, grad_two], axis=0)
    grad_keys = jnp.concatenate([grad_keys, swap(grad_keys)], axis=1)
    grad = lax.dot_general(
        chip_normed, grad_keys, (((0,), (1,)), ((), ())), preferred_element_type=jnp.float32
    )
    return jnp.concatenate(attended, axis=1), scatter_gradient(grad, normed.shape[1] // (2 * CHIPS))


def solution(mesh):
    placed = (
        P("seq", "tp"),
        P("seq", "tp"),
        P("seq", None),
        P("seq", None),
        P("seq", None, "tp"),
        P("tp"),
        P(None, "tp"),
        P(None, "tp"),
    )
    return jax.shard_map(
        per_device,
        mesh=mesh,
        in_specs=placed,
        out_specs=(P("seq", "tp"), P("seq", "tp")),
        check_vma=False,
    )
```

profile of v0, /device:TPU:2, one launch (start us, length us, event | category | flops | bytes accessed | tf_op | source)
XLA Modules:
  0.0 300.4 jit_solution(7211995897012540168)
XLA Ops:
  2.8 16.1 %all_gather.3 = bf16[272,1536]{0,1:T(8,128)(2,1)S(1)} all-gather(bf16[272,384]{0,1:T(8,128)(2,1)S(1)} %fusion.10), channel_id=1, replica_groups=mesh['seq'=64,'tp'=4] {'tp'}, dimensions={1}, use_global_device_ids=true | all-gather | bytes 1044480 | tf_op jit(solution)/shard_map/all_gather | solution.py:251
  25.3 5.9 %collective-permute-start.3 = (bf16[256,512]{1,0:T(8,128)(2,1)S(1)}, bf16[256,512]{1,0:T(8,128)(2,1)S(1)}, u32[]{:S(2)}, u32[]{:S(2)}) collective-permute-start(bf16[256,512]{1,0:T(8,128)(2,1)S(1)} %pad_maximum_fusion.6), channel_id=1, source_target_pairs={{8,0},{12,4},{16,8},{20,12},{24,16},{28,20},{32,24},{36,28},{40,32... | collective-permute-start | bytes 786440 | tf_op jit(solution)/shard_map/one/gather_1/z/ppermute | solution.py:44
  32.0 3.3 %collective-permute-start.15 = (bf16[128,512]{1,0:T(8,128)(2,1)S(1)}, bf16[128,512]{1,0:T(8,128)(2,1)S(1)}, u32[]{:S(2)}, u32[]{:S(2)}) collective-permute-start(bf16[128,512]{1,0:T(8,128)(2,1)S(1)} %slice.240), channel_id=1, source_target_pairs={{64,0},{68,4},{72,8},{76,12},{80,16},{84,20},{88,24},{92,28},{96,3... | collective-permute-start | bytes 393224 | tf_op jit(solution)/shard_map/two/gather_far/y/ppermute | solution.py:39
  35.5 3.6 %collective-permute-start.5 = (bf16[256,512]{1,0:T(8,128)(2,1)S(1)}, bf16[256,512]{1,0:T(8,128)(2,1)S(1)}, u32[]{:S(2)}, u32[]{:S(2)}) collective-permute-start(bf16[256,512]{1,0:T(8,128)(2,1)S(1)} %collective-permute-done.3), channel_id=1, source_target_pairs={{8,0},{12,4},{16,8},{20,12},{24,16},{28,20},{32,24},{36,28},{40,32... | collective-permute-start | bytes 786440 | tf_op jit(solution)/shard_map/one/gather_2/z/ppermute | solution.py:44
  42.5 3.3 %collective-permute-start.17 = (bf16[4,256,512]{2,1,0:T(8,128)(2,1)S(1)}, bf16[4,256,512]{2,1,0:T(8,128)(2,1)S(1)}, u32[]{:S(2)}, u32[]{:S(2)}) collective-permute-start(bf16[4,256,512]{2,1,0:T(8,128)(2,1)S(1)} %pad_maximum_fusion.1.refs_2_), channel_id=1, source_target_pairs={{8,0},{12,4},{16,8},{20,12},{24,16},{28,20},{32,24},{36,28},{40,32... | collective-permute-start | bytes 3145736 | tf_op jit(solution)/shard_map/two/gather_1/z/ppermute | solution.py:44
  51.0 26.0 %collective-permute-done.8 = bf16[256,512]{1,0:T(8,128)(2,1)S(1)} collective-permute-done((bf16[256,512]{1,0:T(8,128)(2,1)S(1)}, bf16[256,512]{1,0:T(8,128)(2,1)S(1)}, u32[]{:S(2)}, u32[]{:S(2)}) %collective-permute-start.8) | collective-permute-done | bytes 262176 | tf_op jit(solution)/shard_map/one/gather_3/z/ppermute | solution.py:44
  95.0 18.1 %collective-permute-done.19.refs_5_ = bf16[4,256,512]{2,1,0:T(8,128)(2,1)} collective-permute-done((bf16[4,256,512]{2,1,0:T(8,128)(2,1)S(1)}, bf16[4,256,512]{2,1,0:T(8,128)(2,1)}, u32[]{:S(2)}, u32[]{:S(2)}) %collective-permute-start.19) | collective-permute-done | bytes 1048608 | tf_op jit(solution)/shard_map/two/gather_2/z/ppermute | solution.py:44
  113.1 3.8 %collective-permute-start.23 = (bf16[4,256,512]{2,1,0:T(8,128)(2,1)}, bf16[4,256,512]{2,1,0:T(8,128)(2,1)S(1)}, u32[]{:S(2)}, u32[]{:S(2)}) collective-permute-start(bf16[4,256,512]{2,1,0:T(8,128)(2,1)} %collective-permute-done.19.refs_5_), channel_id=1, source_target_pairs={{8,0},{12,4},{16,8},{20,12},{24,16},{28,20},{32,24},{36,28},{40,32... | collective-permute-start | bytes 3145736 | tf_op jit(solution)/shard_map/two/gather_3/z/ppermute | solution.py:44
  124.2 10.0 %two_near.1 = (bf16[3072,256]{1,0:T(8,128)(2,1)}, bf16[4,256,256]{2,1,0:T(8,128)(2,1)S(1)}, bf16[4,256,256]{2,1,0:T(8,128)(2,1)S(1)}, bf16[4,256,256]{2,1,0:T(8,...) custom-call(s32[1]{0:T(128)} %bitcast.12.number, s32[48]{0:T(128)S(1)} %get-tuple-element.55.listed, ...), custom_call_target="tpu_custom_call" | custom-call | flops 805306368 | bytes 12582912 | tf_op jit(solution)/shard_map/two_near/pallas_call | solution.py:215
  142.5 10.7 %collective-permute-start.25 = (bf16[2,256,512]{2,1,0:T(8,128)(2,1)S(1)}, bf16[2,256,512]{2,1,0:T(8,128)(2,1)S(1)}, u32[]{:S(2)}, u32[]{:S(2)}) collective-permute-start(bf16[2,256,512]{2,1,0:T(8,128)(2,1)S(1)} %slice.196), channel_id=1, source_target_pairs={{8,0},{12,4},{16,8},{20,12},{24,16},{28,20},{32,24},{36,28},{40,32... | collective-permute-start | bytes 1572872 | tf_op jit(solution)/shard_map/two/gather_far/z/ppermute | solution.py:44
  154.6 11.7 %one_near.1 = (bf16[3072,256]{1,0:T(8,128)(2,1)S(1)}, bf16[8,256,256]{2,1,0:T(8,128)(2,1)S(1)}, bf16[8,256,256]{2,1,0:T(8,128)(2,1)S(1)}, bf16[8,256,256]{2,1,0:T(8,128)(2,1)S(1)}) custom-call(s32[1]{0:T(128)} %bitcast.17.number, s32[48]{0:T(128)S(1)} %get-tuple-element.53.listed, s32[48]{0:T(128)S(1)} %get-tuple-element.52.block, s32[96]{0:T(128)S(1)} %reshape.294.ids, ...), custom_call_target="tpu_custom_call" | custom-call | flops 805306368 | bytes 14155776 | tf_op jit(solution)/shard_map/one_near/pallas_call | solution.py:215
  166.9 9.1 %two_far.1 = (bf16[3072,256]{1,0:T(8,128)(2,1)}, bf16[4,256,256]{2,1,0:T(8,128)(2,1)S(1)}, bf16[4,256,256]{2,1,0:T(8,128)(2,1)S(1)}, bf16[2,256,256]{2,1,0:T(8,128)(2,1)S(1)}, bf16[2,256,256]{2,1,0:T(8,128)(2,1)S(1)}) custom-call(s32[1]{0:T(128)} %bitcast.18.number, s32[48]{0:T(128)S(1)} %get-tuple-element.57.listed, s32[48]{0:T(128)S(1)} %get-tuple-element.56.block, ...), custom_call_target="tpu_custom_call" | custom-call | flops 805306368 | bytes 9437184 | tf_op jit(solution)/shard_map/two_far/pallas_call | solution.py:215
  176.4 5.9 %one_far.1 = (bf16[3072,256]{1,0:T(8,128)(2,1)S(1)}, bf16[4,256,256]{2,1,0:T(8,128)(2,1)S(1)}, bf16[4,256,256]{2,1,0:T(8,128)(2,1)S(1)}) custom-call(s32[1]{0:T(128)} %bitcast.2.number, s32[48]{0:T(128)S(1)} %get-tuple-element.51.listed, s32[48]{0:T(128)S(1)} %get-tuple-element.50.block, s32[96]{0:T(128)S(1)} %reshape.294.ids, ...), custom_call_target="tpu_custom_call" | custom-call | flops 805306368 | bytes 7864320 | tf_op jit(solution)/shard_map/one_far/pallas_call | solution.py:215
  189.2 5.5 %collective-permute-done.46 = bf16[2,256,256]{2,1,0:T(8,128)(2,1)S(1)} collective-permute-done((bf16[2,256,256]{2,1,0:T(8,128)(2,1)S(1)}, bf16[2,256,256]{2,1,0:T(8,128)(2,1)S(1)}, u32[]{:S(2)}, u32[]{:S(2)}) %collective-permute-start.46) | collective-permute-done | bytes 262176 | tf_op jit(solution)/shard_map/two/scatter_far/z/ppermute | solution.py:44
  194.8 3.8 %collective-permute-start.47 = (bf16[4,256,256]{2,1,0:T(8,128)(2,1)S(1)}, bf16[4,256,256]{2,1,0:T(8,128)(2,1)S(1)}, u32[]{:S(2)}, u32[]{:S(2)}) collective-permute-start(bf16[4,256,256]{2,1,0:T(8,128)(2,1)S(1)} %pad_maximum_fusion.5), channel_id=1, source_target_pairs={{8,0},{12,4},{16,8},{20,12},{24,16},{28,20},{32,24},{36,28},{40,32... | collective-permute-start | bytes 1572872 | tf_op jit(solution)/shard_map/two/scatter_3/z/ppermute | solution.py:44
  208.2 3.7 %collective-permute-start.48 = (bf16[4,256,256]{2,1,0:T(8,128)(2,1)}, bf16[4,256,256]{2,1,0:T(8,128)(2,1)}, u32[]{:S(2)}, u32[]{:S(2)}) collective-permute-start(bf16[4,256,256]{2,1,0:T(8,128)(2,1)} %add_convert_fusion.3), channel_id=1, source_target_pairs={{8,0},{12,4},{16,8},{20,12},{24,16},{28,20},{32,24},{36,28},{40,32... | collective-permute-start | bytes 1572872 | tf_op jit(solution)/shard_map/two/scatter_2/z/ppermute | solution.py:44
  211.9 8.2 %collective-permute-done.44 = bf16[4,256,256]{2,1,0:T(8,128)(2,1)} collective-permute-done((bf16[4,256,256]{2,1,0:T(8,128)(2,1)}, bf16[4,256,256]{2,1,0:T(8,128)(2,1)}, u32[]{:S(2)}, u32[]{:S(2)}) %collective-permute-start.44) | collective-permute-done | bytes 524320 | tf_op jit(solution)/shard_map/two/scatter_2/z/ppermute | solution.py:44
  222.8 3.7 %collective-permute-start.49 = (bf16[4,256,256]{2,1,0:T(8,128)(2,1)S(1)}, bf16[4,256,256]{2,1,0:T(8,128)(2,1)S(1)}, u32[]{:S(2)}, u32[]{:S(2)}) collective-permute-start(bf16[4,256,256]{2,1,0:T(8,128)(2,1)S(1)} %add_convert_fusion.2), channel_id=1, source_target_pairs={{8,0},{12,4},{16,8},{20,12},{24,16},{28,20},{32,24},{36,28},{40,32... | collective-permute-start | bytes 1572872 | tf_op jit(solution)/shard_map/two/scatter_1/z/ppermute | solution.py:44
  234.7 3.8 %collective-permute-start.39 = (bf16[256,256]{1,0:T(8,128)(2,1)S(1)}, bf16[256,256]{1,0:T(8,128)(2,1)S(1)}, u32[]{:S(2)}, u32[]{:S(2)}) collective-permute-start(bf16[256,256]{1,0:T(8,128)(2,1)S(1)} %pad_maximum_fusion.10), channel_id=1, source_target_pairs={{8,0},{12,4},{16,8},{20,12},{24,16},{28,20},{32,24},{36,28},{40,32... | collective-permute-start | bytes 393224 | tf_op jit(solution)/shard_map/one/scatter_3/z/ppermute | solution.py:44
  244.9 6.5 %collective-permute-done.36 = bf16[256,256]{1,0:T(8,128)(2,1)S(1)} collective-permute-done((bf16[256,256]{1,0:T(8,128)(2,1)S(1)}, bf16[256,256]{1,0:T(8,128)(2,1)S(1)}, u32[]{:S(2)}, u32[]{:S(2)}) %collective-permute-start.36) | collective-permute-done | bytes 131104 | tf_op jit(solution)/shard_map/one/scatter_2/z/ppermute | solution.py:44
  265.5 3.5 %all-to-all-start = ((bf16[4,8,24,512]{3,2,1,0:T(8,128)(2,1)}), bf16[4,8,24,512]{3,2,1,0:T(8,128)(2,1)S(1)}, u32[]{:S(2)}, u32[]{:S(2)}) async-start(bf16[4,8,24,512]{3,2,1,0:T(8,128)(2,1)} %bitcast.138), calls=%async_computation | async-start | bytes 1572864 | tf_op jit(solution)/shard_map/all_to_all | solution.py:267
  269.2 13.0 %all-to-all-done = bf16[4,8,24,512]{3,2,1,0:T(8,128)(2,1)S(1)} async-done(((bf16[4,8,24,512]{3,2,1,0:T(8,128)(2,1)}), bf16[4,8,24,512]{3,2,1,0:T(8,128)(2,1)S(1)}, u32[]{:S(2)}, u32[]{:S(2)}) %all-to-all-start) | async-done | bytes 786464 | tf_op jit(solution)/shard_map/all_to_all | solution.py:267
  283.0 6.3 %all-to-all-start.1 = ((bf16[8,1,24,512]{3,2,1,0:T(8,128)(2,1)}), bf16[8,1,24,512]{3,2,1,0:T(8,128)(2,1)S(1)}, u32[]{:S(2)}, u32[]{:S(2)}) async-start(bf16[8,1,24,512]{3,2,1,0:T(8,128)(2,1)} %bitcast.42), calls=%async_computation.1 | async-start | bytes 393216 | tf_op jit(solution)/shard_map/all_to_all | solution.py:267
  292.6 6.7 %all-to-all-done.1 = bf16[8,1,24,512]{3,2,1,0:T(8,128)(2,1)S(1)} async-done(((bf16[8,1,24,512]{3,2,1,0:T(8,128)(2,1)}), bf16[8,1,24,512]{3,2,1,0:T(8,128)(2,1)S(1)}, u32[]{:S(2)}, u32[]{:S(2)}) %all-to-all-start.1) | async-done | bytes 196640 | tf_op jit(solution)/shard_map/all_to_all | solution.py:267
  (236 shorter events, 106.4 us)
Async XLA Ops:
  31.3 59.0 %collective-permute-start.1 = (bf16[1536,512]{1,0:T(8,128)(2,1)S(1)}, bf16[1536,512]{1,0:T(8,128)(2,1)}, u32[]{:S(2)}, u32[]{:S(2)}) collective-permute-start(bf16[1536,512]{1,0:T(8,128)(2,1)S(1)} %copy-done.17), channel_id=1, source_target_pairs={{0,4},{4,0},{8,12},{12,8},{16,20},{20,16},{24,28},{28,24},{32,36},... | collective-permute-start | bytes 4718600 | tf_op jit(solution)/shard_map/swap/ppermute | solution.py:34
  42.5 44.9 %collective-permute-start.17 = (bf16[4,256,512]{2,1,0:T(8,128)(2,1)S(1)}, bf16[4,256,512]{2,1,0:T(8,128)(2,1)S(1)}, u32[]{:S(2)}, u32[]{:S(2)}) collective-permute-start(bf16[4,256,512]{2,1,0:T(8,128)(2,1)S(1)} %pad_maximum_fusion.1.refs_2_), channel_id=1, source_target_pairs={{8,0},{12,4},{16,8},{20,12},{24,16},{28,20},{32,24},{36,28},{40,32... | collective-permute-start | bytes 3145736 | tf_op jit(solution)/shard_map/two/gather_1/z/ppermute | solution.py:44
  45.8 41.6 %collective-permute-start.18 = (bf16[4,256,512]{2,1,0:T(8,128)(2,1)S(1)}, bf16[4,256,512]{2,1,0:T(8,128)(2,1)S(1)}, u32[]{:S(2)}, u32[]{:S(2)}) collective-permute-start(bf16[4,256,512]{2,1,0:T(8,128)(2,1)S(1)} %pad_maximum_fusion.1.refs_2_), channel_id=1, source_target_pairs={{56,0},{60,4},{0,8},{4,12},{8,16},{12,20},{16,24},{20,28},{24,32},... | collective-permute-start | bytes 3145736 | tf_op jit(solution)/shard_map/two/gather_1/z/ppermute | solution.py:44
  45.8 31.3 %collective-permute-start.7 = (bf16[256,512]{1,0:T(8,128)(2,1)S(1)}, bf16[256,512]{1,0:T(8,128)(2,1)S(1)}, u32[]{:S(2)}, u32[]{:S(2)}) collective-permute-start(bf16[256,512]{1,0:T(8,128)(2,1)S(1)} %collective-permute-done.5), channel_id=1, source_target_pairs={{8,0},{12,4},{16,8},{20,12},{24,16},{28,20},{32,24},{36,28},{40,32... | collective-permute-start | bytes 786440 | tf_op jit(solution)/shard_map/one/gather_3/z/ppermute | solution.py:44
  49.3 27.7 %collective-permute-start.8 = (bf16[256,512]{1,0:T(8,128)(2,1)S(1)}, bf16[256,512]{1,0:T(8,128)(2,1)S(1)}, u32[]{:S(2)}, u32[]{:S(2)}) collective-permute-start(bf16[256,512]{1,0:T(8,128)(2,1)S(1)} %collective-permute-done.6), channel_id=1, source_target_pairs={{56,0},{60,4},{0,8},{4,12},{8,16},{12,20},{16,24},{20,28},{24,32},... | collective-permute-start | bytes 786440 | tf_op jit(solution)/shard_map/one/gather_3/z/ppermute | solution.py:44
  83.2 37.7 %collective-permute-start.2 = (bf16[1536,512]{1,0:T(8,128)(2,1)}, bf16[1536,512]{1,0:T(8,128)(2,1)}, u32[]{:S(2)}, u32[]{:S(2)}) collective-permute-start(bf16[1536,512]{1,0:T(8,128)(2,1)} %param.9), channel_id=1, source_target_pairs={{0,4},{4,0},{8,12},{12,8},{16,20},{20,16},{24,28},{28,24},{32,36},... | collective-permute-start | bytes 4718600 | tf_op jit(solution)/shard_map/swap/ppermute | solution.py:34
  84.5 49.7 %collective-permute-start.11 = (bf16[8,256,512]{2,1,0:T(8,128)(2,1)}, bf16[8,256,512]{2,1,0:T(8,128)(2,1)}, u32[]{:S(2)}, u32[]{:S(2)}) collective-permute-start(bf16[8,256,512]{2,1,0:T(8,128)(2,1)} %fusion.11.refs_2_), channel_id=1, source_target_pairs={{64,0},{68,4},{72,8},{76,12},{80,16},{84,20},{88,24},{92,28},{96,3... | collective-permute-start | bytes 6291464 | tf_op jit(solution)/shard_map/one/gather_1/y/ppermute | solution.py:39
  87.3 48.9 %collective-permute-start.12 = (bf16[8,256,512]{2,1,0:T(8,128)(2,1)}, bf16[8,256,512]{2,1,0:T(8,128)(2,1)}, u32[]{:S(2)}, u32[]{:S(2)}) collective-permute-start(bf16[8,256,512]{2,1,0:T(8,128)(2,1)} %fusion.11.refs_2_), channel_id=1, source_target_pairs={{192,0},{196,4},{200,8},{204,12},{208,16},{212,20},{216,24},{220,2... | collective-permute-start | bytes 6291464 | tf_op jit(solution)/shard_map/one/gather_1/y/ppermute | solution.py:39
  87.4 25.7 %collective-permute-start.19 = (bf16[4,256,512]{2,1,0:T(8,128)(2,1)S(1)}, bf16[4,256,512]{2,1,0:T(8,128)(2,1)}, u32[]{:S(2)}, u32[]{:S(2)}) collective-permute-start(bf16[4,256,512]{2,1,0:T(8,128)(2,1)S(1)} %collective-permute-done.17.refs_3_), channel_id=1, source_target_pairs={{8,0},{12,4},{16,8},{20,12},{24,16},{28,20},{32,24},{36,28},{40,32... | collective-permute-start | bytes 3145736 | tf_op jit(solution)/shard_map/two/gather_2/z/ppermute | solution.py:44
  90.3 26.6 %collective-permute-start.20 = (bf16[4,256,512]{2,1,0:T(8,128)(2,1)S(1)}, bf16[4,256,512]{2,1,0:T(8,128)(2,1)}, u32[]{:S(2)}, u32[]{:S(2)}) collective-permute-start(bf16[4,256,512]{2,1,0:T(8,128)(2,1)S(1)} %collective-permute-done.18.refs_4_), channel_id=1, source_target_pairs={{56,0},{60,4},{0,8},{4,12},{8,16},{12,20},{16,24},{20,28},{24,32},... | collective-permute-start | bytes 3145736 | tf_op jit(solution)/shard_map/two/gather_2/z/ppermute | solution.py:44
  113.1 27.9 %collective-permute-start.23 = (bf16[4,256,512]{2,1,0:T(8,128)(2,1)}, bf16[4,256,512]{2,1,0:T(8,128)(2,1)S(1)}, u32[]{:S(2)}, u32[]{:S(2)}) collective-permute-start(bf16[4,256,512]{2,1,0:T(8,128)(2,1)} %collective-permute-done.19.refs_5_), channel_id=1, source_target_pairs={{8,0},{12,4},{16,8},{20,12},{24,16},{28,20},{32,24},{36,28},{40,32... | collective-permute-start | bytes 3145736 | tf_op jit(solution)/shard_map/two/gather_3/z/ppermute | solution.py:44
  116.9 25.6 %collective-permute-start.24 = (bf16[4,256,512]{2,1,0:T(8,128)(2,1)}, bf16[4,256,512]{2,1,0:T(8,128)(2,1)S(1)}, u32[]{:S(2)}, u32[]{:S(2)}) collective-permute-start(bf16[4,256,512]{2,1,0:T(8,128)(2,1)} %collective-permute-done.20.refs_6_), channel_id=1, source_target_pairs={{56,0},{60,4},{0,8},{4,12},{8,16},{12,20},{16,24},{20,28},{24,32},... | collective-permute-start | bytes 3145736 | tf_op jit(solution)/shard_map/two/gather_3/z/ppermute | solution.py:44
  137.5 38.9 %collective-permute-start.21 = (bf16[4,256,512]{2,1,0:T(8,128)(2,1)S(1)}, bf16[4,256,512]{2,1,0:T(8,128)(2,1)S(1)}, u32[]{:S(2)}, u32[]{:S(2)}) collective-permute-start(bf16[4,256,512]{2,1,0:T(8,128)(2,1)S(1)} %slice.194), channel_id=1, source_target_pairs={{64,0},{68,4},{72,8},{76,12},{80,16},{84,20},{88,24},{92,28},{96,3... | collective-permute-start | bytes 3145736 | tf_op jit(solution)/shard_map/one/gather_far/y/ppermute | solution.py:39
  140.3 36.1 %collective-permute-start.22 = (bf16[4,256,512]{2,1,0:T(8,128)(2,1)S(1)}, bf16[4,256,512]{2,1,0:T(8,128)(2,1)S(1)}, u32[]{:S(2)}, u32[]{:S(2)}) collective-permute-start(bf16[4,256,512]{2,1,0:T(8,128)(2,1)S(1)} %slice.195), channel_id=1, source_target_pairs={{192,0},{196,4},{200,8},{204,12},{208,16},{212,20},{216,24},{220,2... | collective-permute-start | bytes 3145736 | tf_op jit(solution)/shard_map/one/gather_far/y/ppermute | solution.py:39
  142.5 23.8 %collective-permute-start.25 = (bf16[2,256,512]{2,1,0:T(8,128)(2,1)S(1)}, bf16[2,256,512]{2,1,0:T(8,128)(2,1)S(1)}, u32[]{:S(2)}, u32[]{:S(2)}) collective-permute-start(bf16[2,256,512]{2,1,0:T(8,128)(2,1)S(1)} %slice.196), channel_id=1, source_target_pairs={{8,0},{12,4},{16,8},{20,12},{24,16},{28,20},{32,24},{36,28},{40,32... | collective-permute-start | bytes 1572872 | tf_op jit(solution)/shard_map/two/gather_far/z/ppermute | solution.py:44
  182.3 16.3 %collective-permute-start.30 = (bf16[4,256,256]{2,1,0:T(8,128)(2,1)S(1)}, bf16[4,256,256]{2,1,0:T(8,128)(2,1)S(1)}, u32[]{:S(2)}, u32[]{:S(2)}) collective-permute-start(bf16[4,256,256]{2,1,0:T(8,128)(2,1)S(1)} %get-tuple-element.38), channel_id=1, source_target_pairs={{192,0},{196,4},{200,8},{204,12},{208,16},{212,20},{216,24},{220,2... | collective-permute-start | bytes 1572872 | tf_op jit(solution)/shard_map/one/scatter_far/y/ppermute | solution.py:39
  199.8 26.6 %collective-permute-start.31 = (bf16[8,256,256]{2,1,0:T(8,128)(2,1)}, bf16[8,256,256]{2,1,0:T(8,128)(2,1)}, u32[]{:S(2)}, u32[]{:S(2)}) collective-permute-start(bf16[8,256,256]{2,1,0:T(8,128)(2,1)} %pad_maximum_fusion.2), channel_id=1, source_target_pairs={{192,0},{196,4},{200,8},{204,12},{208,16},{212,20},{216,24},{220,2... | collective-permute-start | bytes 3145736 | tf_op jit(solution)/shard_map/one/scatter_1/y/ppermute | solution.py:39
  201.0 25.4 %collective-permute-start.33 = (bf16[8,256,256]{2,1,0:T(8,128)(2,1)}, bf16[8,256,256]{2,1,0:T(8,128)(2,1)}, u32[]{:S(2)}, u32[]{:S(2)}) collective-permute-start(bf16[8,256,256]{2,1,0:T(8,128)(2,1)} %pad_maximum_fusion.3), channel_id=1, source_target_pairs={{64,0},{68,4},{72,8},{76,12},{80,16},{84,20},{88,24},{92,28},{96,3... | collective-permute-start | bytes 3145736 | tf_op jit(solution)/shard_map/one/scatter_1/y/ppermute | solution.py:39
  221.5 17.1 %collective-permute-start.45 = (bf16[4,256,256]{2,1,0:T(8,128)(2,1)S(1)}, bf16[4,256,256]{2,1,0:T(8,128)(2,1)S(1)}, u32[]{:S(2)}, u32[]{:S(2)}) collective-permute-start(bf16[4,256,256]{2,1,0:T(8,128)(2,1)S(1)} %add_convert_fusion.4), channel_id=1, source_target_pairs={{56,0},{60,4},{0,8},{4,12},{8,16},{12,20},{16,24},{20,28},{24,32},... | collective-permute-start | bytes 1572872 | tf_op jit(solution)/shard_map/two/scatter_1/z/ppermute | solution.py:44
  231.9 32.1 %collective-permute-start.29 = (bf16[256,32,24]{0,2,1:T(8,128)(2,1)S(1)}, bf16[256,32,24]{0,2,1:T(8,128)(2,1)S(1)}, u32[]{:S(2)}, u32[]{:S(2)}) collective-permute-start(bf16[256,32,24]{0,2,1:T(8,128)(2,1)S(1)} %get-tuple-element.81), channel_id=1, source_target_pairs={{0,4},{4,0},{8,12},{12,8},{16,20},{20,16},{24,28},{28,24},{32,36},... | collective-permute-start | bytes 1179656 | tf_op jit(solution)/shard_map/swap/ppermute | solution.py:34
  263.5 25.8 %collective-permute-start.27 = (bf16[1536,256]{1,0:T(8,128)(2,1)}, bf16[1536,256]{1,0:T(8,128)(2,1)}, u32[]{:S(2)}, u32[]{:S(2)}) collective-permute-start(bf16[1536,256]{1,0:T(8,128)(2,1)} %slice.199), channel_id=1, source_target_pairs={{0,4},{4,0},{8,12},{12,8},{16,20},{20,16},{24,28},{28,24},{32,36},... | collective-permute-start | bytes 2359304 | tf_op jit(solution)/shard_map/swap/ppermute | solution.py:34
  264.0 25.3 %collective-permute-start.28 = (bf16[1536,256]{1,0:T(8,128)(2,1)S(1)}, bf16[1536,256]{1,0:T(8,128)(2,1)}, u32[]{:S(2)}, u32[]{:S(2)}) collective-permute-start(bf16[1536,256]{1,0:T(8,128)(2,1)S(1)} %slice.201), channel_id=1, source_target_pairs={{0,4},{4,0},{8,12},{12,8},{16,20},{20,16},{24,28},{28,24},{32,36},... | collective-permute-start | bytes 2359304 | tf_op jit(solution)/shard_map/swap/ppermute | solution.py:34
  265.5 16.7 %all-to-all-start = ((bf16[4,8,24,512]{3,2,1,0:T(8,128)(2,1)}), bf16[4,8,24,512]{3,2,1,0:T(8,128)(2,1)S(1)}, u32[]{:S(2)}, u32[]{:S(2)}) async-start(bf16[4,8,24,512]{3,2,1,0:T(8,128)(2,1)} %bitcast.138), calls=%async_computation | async-start | bytes 1572864 | tf_op jit(solution)/shard_map/all_to_all | solution.py:267
  283.0 16.3 %all-to-all-start.1 = ((bf16[8,1,24,512]{3,2,1,0:T(8,128)(2,1)}), bf16[8,1,24,512]{3,2,1,0:T(8,128)(2,1)S(1)}, u32[]{:S(2)}, u32[]{:S(2)}) async-start(bf16[8,1,24,512]{3,2,1,0:T(8,128)(2,1)} %bitcast.42), calls=%async_computation.1 | async-start | bytes 393216 | tf_op jit(solution)/shard_map/all_to_all | solution.py:267
  (54 other events, 487.0 us)
where the time goes:
time: 306 us; the launch traced here: 300 us
  waiting for transfers between devices  102 us (33%)
  starting transfers between devices  98.7 us (32%)
  Pallas kernels  36.7 us (12%)
  other arithmetic  21.2 us (7%)
  local copies, waits for them, and re-layouts  20.9 us (7%)
  blocking collectives  16.1 us (5%)
    ppermute x32, waiting for transfers between devices, from_z(): lax.ppermute(x, 'seq', [(seq_of(y, z + step, c), seq_of(y, z, c)) for y,...  78.8 us
    ppermute x32, starting transfers between devices, from_z(): lax.ppermute(x, 'seq', [(seq_of(y, z + step, c), seq_of(y, z, c)) for y,...  63.1 us
    pallas_call x4, Pallas kernels, attend(): pl.pallas_call(functools.partial(attention_kernel, heads, sizes, bool(bef...  36.7 us
    ppermute x16, starting transfers between devices, from_y(): lax.ppermute(x, 'seq', [(seq_of(y + step, z, c), seq_of(y, z, c)) for y,...  24.6 us
    all_to_all x2, waiting for transfers between devices, scatter_gradient(): lax.all_to_all(total, 'seq', 0, 0, axis_index_groups=groups, tiled=True)  19.7 us
    all_gather x1, blocking collectives, normed_store(): whole = lax.all_gather(packed, 'tp', axis=1, tiled=True).astype(jnp.float32)  16.1 us
    unnamed x51, local copies, waits for them, and re-layouts  10.9 us
    all_to_all x2, starting transfers between devices, scatter_gradient(): lax.all_to_all(total, 'seq', 0, 0, axis_index_groups=groups, tiled=True)  9.78 us
  transfers between devices with their start and end apart: 57, of which 19 were waited for; matrix products, arithmetic and copies ran while one was open for 12% of the time, Pallas kernels for 12%

commit v1 on v0

v1 whole, which is shorter than its diff:
```python
import functools
import math

import jax
import jax.numpy as jnp
from jax import lax
from jax.experimental import pallas as pl
from jax.experimental.pallas import tpu as pltpu
from jax.sharding import PartitionSpec as P

D_HEAD = 128
SPAN = 64
NLEN = 128
N_Y, N_Z = 4, 8
CHIPS = N_Y * N_Z
TOGETHER = 2
epsilon = 1e-06


def seq_of(y, z, core):
    return ((y % N_Y) * N_Z + z % N_Z) * 2 + core


PAIR = [(i, i ^ 1) for i in range(2 * CHIPS)]
Z_GROUPS = [[seq_of(y, z, c) for z in range(N_Z)] for y in range(N_Y) for c in range(2)]
Y_GROUPS = [[seq_of(y, z, c) for y in range(N_Y)] for z in range(N_Z) for c in range(2)]
LINES = [[seq_of(y, z, c) for y in range(N_Y) for c in range(2)] for z in range(N_Z)]
CELLS = [(y, z, c) for y in range(N_Y) for z in range(N_Z) for c in range(2)]
NT = (((1,), (1,)), ((), ()))
TN = (((0,), (0,)), ((), ()))


def swap(x):
    with jax.named_scope("swap"):
        return lax.ppermute(x, "seq", PAIR)


def from_y(x, step):
    with jax.named_scope("y"):
        return lax.ppermute(x, "seq", [(seq_of(y + step, z, c), seq_of(y, z, c)) for y, z, c in CELLS])


def from_z(x, step):
    with jax.named_scope("z"):
        return lax.ppermute(x, "seq", [(seq_of(y, z + step, c), seq_of(y, z, c)) for y, z, c in CELLS])


def add(x, *others):
    total = x.astype(jnp.float32)
    for other in others:
        total = total + other.astype(jnp.float32)
    return total.astype(jnp.bfloat16)


def after(values, done):
    return lax.optimization_barrier((values, done))[0]


def halves(x):
    middle = x.shape[0] // 2
    return x[:middle], x[middle:]


def ring_near(x, fetch, size):
    up, down, parts = x, x, [x]
    for hop in range(1, size // 2):
        with jax.named_scope(f"gather_{hop}"):
            up, down = fetch(up, 1), fetch(down, -1)
        parts += [up, down]
    return parts


def ring_far(parts, fetch):
    with jax.named_scope("gather_far"):
        return [fetch(halves(parts[-2])[0], 1), fetch(halves(parts[-1])[1], -1)]


def ring_scatter(parts, fetch, size):
    plus, minus = parts[size - 3], parts[size - 2]
    with jax.named_scope("scatter_far"):
        if len(parts) == size:
            plus = add(plus, fetch(parts[-1], -1))
        else:
            first, second = fetch(parts[-2], -1), fetch(parts[-1], 1)
            plus = jnp.concatenate([add(halves(plus)[0], first), halves(plus)[1]])
            minus = jnp.concatenate([halves(minus)[0], add(halves(minus)[1], second)])
    for hop in range(size // 2 - 2, 0, -1):
        with jax.named_scope(f"scatter_{hop + 1}"):
            plus, minus = (
                add(parts[2 * hop - 1], fetch(plus, -1)),
                add(parts[2 * hop], fetch(minus, 1)),
            )
    with jax.named_scope("scatter_1"):
        return add(parts[0], fetch(plus, -1), fetch(minus, 1))


def ring_place(offset, size):
    offset = offset % size
    place = jnp.where(offset < size // 2, 2 * offset - 1, 2 * (size - offset))
    place = jnp.where(offset == size // 2, size - 1, place)
    return jnp.where(offset == 0, 0, place)


def work_list(place, chosen):
    order = jnp.arange(place.shape[0])
    before = order[None, :] < order[:, None]
    rank = jnp.sum((before & chosen[None, :]).astype(jnp.int32), axis=1)
    at = chosen[None, :] & (rank[None, :] == order[:, None])
    listed = jnp.sum(jnp.where(at, order[None, :], 0), axis=1).astype(jnp.int32)
    block = jnp.sum(jnp.where(at, place[None, :], 0), axis=1).astype(jnp.int32)
    return jnp.sum(chosen.astype(jnp.int32)).reshape(1), listed, block


def attention_kernel(heads, last, number, listed, block, ids, spans, *refs):
    taken = N_Z + 1 + last
    sources, refs = refs[:taken], refs[taken:]
    qc, kv, acc, att, semaphores = refs[-5:]
    out, grad_outs = refs[0], refs[1:-5]
    inv_root = 1.0 / math.sqrt(D_HEAD)
    dot = functools.partial(lax.dot_general, preferred_element_type=jnp.float32)
    devices, tokens = out.shape[:2]

    moves = [
        (spans.at[i, pl.ds(j * tokens, tokens)], qc.at[j, pl.ds(i * tokens, tokens)])
        for i in range(devices)
        for j in range(2)
    ]
    for i, source in enumerate(sources[: N_Z - 1]):
        moves.append((source, kv.at[i]))
    for i, source in enumerate(sources[N_Z - 1 : N_Z + 1]):
        moves.append((source, kv.at[N_Z - 1, pl.ds(i * NLEN, NLEN)]))
    if last:
        moves.append((sources[-1], acc))
    copies = [
        pltpu.make_async_copy(source, target, semaphores.at[i])
        for i, (source, target) in enumerate(moves)
    ]
    for copy in copies:
        copy.start()
    if not last:
        acc[...] = jnp.zeros_like(acc)
    att[...] = jnp.zeros_like(att)
    for copy in copies:
        copy.wait()

    first_half = lax.broadcasted_iota(jnp.int32, (1, 2 * NLEN), 1) < NLEN
    amount = number[0]
    width = heads * D_HEAD
    key_cols = [slice(h * D_HEAD, (h + 1) * D_HEAD) for h in range(heads)]
    value_cols = [slice(width + h * D_HEAD, width + (h + 1) * D_HEAD) for h in range(heads)]

    def step(i, carry):
        items = []
        for u in range(TOGETHER):
            k = i * TOGETHER + u
            at = jnp.minimum(k, amount - 1)
            span, place = listed[at], block[at]
            rows = pl.ds(pl.multiple_of(span * SPAN, SPAN), SPAN)
            one, two = ids[2 * span], ids[2 * span + 1]
            low = jnp.where((one == 0) | (two == 0), 0.0, -1e30)
            high = jnp.where((one == 1) | (two == 1), 0.0, -1e30)
            bias = jnp.where(first_half, low, high)
            scale = jnp.where(k < amount, inv_root, 0.0)
            items += [(rows, place, bias, scale, h) for h in range(heads)]
        q = [qc[0, rows, key_cols[h]] for rows, _, _, _, h in items]
        scores = [
            dot(x, kv[place, :, key_cols[h]], NT) * (inv_root * math.log2(math.e)) + bias
            for x, (_, place, bias, _, h) in zip(q, items)
        ]
        grad_probs = [
            dot(qc[1, rows, key_cols[h]], kv[place, :, value_cols[h]], NT)
            for rows, place, _, _, h in items
        ]
        highest = [jnp.max(s, axis=1, keepdims=True) for s in scores]
        weights = [jnp.exp2(s - m) for s, m in zip(scores, highest)]
        sums = [jnp.sum(w, axis=1, keepdims=True) for w in weights]
        probs = [w * (1.0 / s) for w, s in zip(weights, sums)]
        deltas = [jnp.sum(p * g, axis=1, keepdims=True) for p, g in zip(probs, grad_probs)]
        grad_scores = [
            (p * (g - d) * item[3]).astype(jnp.bfloat16)
            for p, g, d, item in zip(probs, grad_probs, deltas, items)
        ]
        for p, (rows, place, _, _, h) in zip(probs, items):
            out = jnp.dot(
                p.astype(jnp.bfloat16),
                kv[place, :, value_cols[h]],
                preferred_element_type=jnp.float32,
            )
            att[rows, key_cols[h]] = out.astype(jnp.bfloat16)
        for x, g, (_, place, _, _, h) in zip(q, grad_scores, items):
            acc[place, key_cols[h]] += dot(x, g, TN)
        return carry

    lax.fori_loop(0, (amount + TOGETHER - 1) // TOGETHER, step, 0)

    copies = [
        pltpu.make_async_copy(att.at[pl.ds(i * tokens, tokens)], out.at[i], semaphores.at[i])
        for i in range(devices)
    ]
    if not last:
        copies.append(pltpu.make_async_copy(acc, grad_outs[0], semaphores.at[devices]))
    for copy in copies:
        copy.start()
    if last:
        for i, ref in enumerate(grad_outs[: N_Z - 1]):
            ref[...] = acc[i].astype(jnp.bfloat16)
        for i, ref in enumerate(grad_outs[N_Z - 1 :]):
            ref[...] = acc[N_Z - 1, i * width // 2 : (i + 1) * width // 2].astype(jnp.bfloat16)
    for copy in copies:
        copy.wait()


def attend(work, ids, spans, tokens, parts, earlier=None):
    seen, width = parts[0].shape[0], parts[0].shape[1] // 2
    heads, last, devices = width // D_HEAD, earlier is not None, spans.shape[0]
    rows = devices * tokens
    operands = [spans, *parts] + ([earlier] if last else [])
    anywhere = pl.BlockSpec(memory_space=pl.ANY)
    sums = jax.ShapeDtypeStruct((N_Z, width, seen), jnp.float32)
    shapes = [(width, seen)] * (N_Z - 1) + [(width // 2, seen)] * 2
    out = pl.pallas_call(
        functools.partial(attention_kernel, heads, last),
        grid_spec=pltpu.PrefetchScalarGridSpec(
            num_scalar_prefetch=4,
            grid=(1,),
            in_specs=[anywhere] * len(operands),
            out_specs=[anywhere]
            + ([pl.BlockSpec(shape, lambda i, *_: (0, 0)) for shape in shapes] if last else [anywhere]),
            scratch_shapes=[
                pltpu.VMEM((2, rows, width), jnp.bfloat16),
                pltpu.VMEM((N_Z, seen, 2 * width), jnp.bfloat16),
                pltpu.VMEM((N_Z, width, seen), jnp.float32),
                pltpu.VMEM((rows, width), jnp.bfloat16),
                pltpu.SemaphoreType.DMA((2 * devices + N_Z + 2,)),
            ],
        ),
        out_shape=[jax.ShapeDtypeStruct((devices, tokens, width), jnp.bfloat16)]
        + ([jax.ShapeDtypeStruct(shape, jnp.bfloat16) for shape in shapes] if last else [sums]),
        compiler_params=pltpu.CompilerParams(vmem_limit_bytes=50 * 1024 * 1024),
        cost_estimate=pl.CostEstimate(
            flops=rows * seen * width * 2,
            bytes_accessed=rows * width * 6 + N_Z * seen * width * 10,
            transcendentals=rows * seen * heads // 4,
        ),
    )(*work, ids, *operands)
    return out[0], list(out[1:])


def normed_store(database, norm_gain):
    rows = database.reshape(-1, database.shape[2])
    stored = rows.shape[0]
    top = lax.reduce_precision(norm_gain, 8, 7)
    middle = lax.reduce_precision(norm_gain - top, 8, 7)
    bottom = norm_gain - top - middle
    gains = jnp.stack([top, middle, bottom]).astype(jnp.bfloat16)
    packed = jnp.concatenate([rows, jnp.pad(gains, ((0, 13), (0, 0)))], axis=0)
    whole = lax.all_gather(packed, "tp", axis=1, tiled=True).astype(jnp.float32)
    floats = whole[:stored]
    gain = whole[stored] + whole[stored + 1] + whole[stored + 2]
    mean = jnp.sum(floats * floats, axis=1, keepdims=True) / floats.shape[1]
    return (floats * lax.rsqrt(mean + epsilon) * gain[None, :]).astype(jnp.bfloat16)


def core_rows(x, core):
    return lax.dynamic_index_in_dim(x.reshape(x.shape[0], CHIPS, 2, -1), core, 2, False)


def scatter_gradient(total, rows):
    width = total.shape[1]
    for groups in (Y_GROUPS, Z_GROUPS):
        size = len(groups[0])
        total = total.astype(jnp.bfloat16).reshape(size, -1, rows, width)
        total = lax.all_to_all(total, "seq", 0, 0, axis_index_groups=groups, tiled=True)
        total = jnp.sum(total.astype(jnp.float32), axis=0)
    return total.reshape(rows, width)


def per_device(
    queries, cotangent, owner_map, neighbour_ids, database, norm_gain, key_weight, value_weight
):
    index = lax.axis_index("seq")
    core, here_y, here_z = index % 2, index // (2 * N_Z), index // 2 % N_Z
    tokens, local_width = queries.shape

    half = tokens // 2
    with jax.named_scope("spans"):
        meta = jnp.concatenate([owner_map, neighbour_ids], axis=1).T.astype(jnp.bfloat16)
        meta = meta.reshape(3, 2, -1)
        meta = jnp.pad(meta, ((0, 13), (0, 0), (0, local_width - meta.shape[2])))
        lines = []
        for i in range(2):
            rows = slice(i * half, (i + 1) * half)
            line = jnp.concatenate([queries[rows], cotangent[rows], meta[:, i]], axis=0)
            lines.append(lax.all_gather(line, "seq", axis_index_groups=LINES, axis=0, tiled=False))

    normed = normed_store(database, norm_gain)
    key_rows = jnp.dot(normed, key_weight, preferred_element_type=jnp.float32).astype(jnp.bfloat16)
    value_rows = jnp.dot(normed, value_weight, preferred_element_type=jnp.float32).astype(
        jnp.bfloat16
    )

    chip_normed = [core_rows(normed, core), swap(core_rows(normed, 1 - core))]
    chip_normed = jnp.concatenate(chip_normed, axis=0).reshape(2 * normed.shape[0], -1)

    with jax.named_scope("keys_values"):
        kv = jnp.concatenate([key_rows, value_rows], axis=1)
        kv = ring_near(kv, from_z, N_Z)
        kv += ring_far(kv, from_z)

    sums, attended = None, []
    for line in lines:
        if sums is not None:
            line = after(line, sums[0])
        meta = line[:, tokens : tokens + 3, : half // SPAN].astype(jnp.int32)
        owners, ids = meta[:, 0].reshape(-1), meta[:, 1:].transpose(0, 2, 1).reshape(-1)
        member = (owners % 2 == core) & (owners // (2 * N_Z) == here_y)
        work = work_list(ring_place(owners // 2 - here_z, N_Z), member)
        with jax.named_scope("attend"):
            att, sums = attend(work, ids, line, half, kv, None if sums is None else sums[0])
        with jax.named_scope("attended"):
            attended.append(
                lax.psum_scatter(att, "seq", axis_index_groups=LINES, scatter_dimension=0, tiled=False)
            )
    with jax.named_scope("key_gradients"):
        grad_keys = ring_scatter(sums, from_z, N_Z)

    grad_keys = jnp.concatenate([grad_keys, swap(grad_keys)], axis=1)
    grad = lax.dot_general(
        chip_normed, grad_keys, (((0,), (1,)), ((), ())), preferred_element_type=jnp.float32
    )
    grad = scatter_gradient(grad, normed.shape[1] // (2 * CHIPS))
    return jnp.concatenate(attended, axis=0), grad


def solution(mesh):
    placed = (
        P("seq", "tp"),
        P("seq", "tp"),
        P("seq", None),
        P("seq", None),
        P("seq", None, "tp"),
        P("tp"),
        P(None, "tp"),
        P(None, "tp"),
    )
    return jax.shard_map(
        per_device,
        mesh=mesh,
        in_specs=placed,
        out_specs=(P("seq", "tp"), P("seq", "tp")),
        check_vma=False,
    )
```

time: 306 us -> 272 us (0.89); the launches traced: 300 us -> 271 us
  starting transfers between devices: 98.7 us -> 31.3 us
  blocking collectives: 16.1 us -> 55.2 us
  waiting for transfers between devices: 102 us -> 120 us
  local copies, waits for them, and re-layouts: 20.9 us -> 7.53 us
  between operations: 1.92 us -> 14.2 us
  other arithmetic: 21.2 us -> 12.8 us
  Pallas kernels: 36.7 us -> 28.6 us
    all_gather x0 -> x2, waiting for transfers between devices: none -> 64.5 us  [per_device(): lax.all_gather(line, 'seq', axis_index_groups=LINES, axis=0, tiled=False)]
    all_to_all x0 -> x2, blocking collectives: none -> 39.1 us  [scatter_gradient(): lax.all_to_all(total, 'seq', 0, 0, axis_index_groups=groups, tiled=True)]
    ppermute x32 -> x16, waiting for transfers between devices: 78.8 us -> 44.1 us  [from_z(): lax.ppermute(x, 'seq', [(seq_of(y, z + step, c), seq_of(y, z, c)) for y,...]
    ppermute x32 -> x16, starting transfers between devices: 63.1 us -> 30.7 us  [from_z(): lax.ppermute(x, 'seq', [(seq_of(y, z + step, c), seq_of(y, z, c)) for y,...]
    ppermute x16 -> x0, starting transfers between devices: 24.6 us -> none  [from_y(): lax.ppermute(x, 'seq', [(seq_of(y + step, z, c), seq_of(y, z, c)) for y,...]
    all_to_all x2 -> x0, waiting for transfers between devices: 19.7 us -> none  [scatter_gradient(): lax.all_to_all(total, 'seq', 0, 0, axis_index_groups=groups, tiled=True)]
    reduce_scatter x0 -> x2, waiting for transfers between devices: none -> 9.93 us  [per_device(): lax.psum_scatter(att, 'seq', axis_index_groups=LINES, scatter_dimension=0...]
    all_to_all x2 -> x0, starting transfers between devices: 9.78 us -> none  [scatter_gradient(): lax.all_to_all(total, 'seq', 0, 0, axis_index_groups=groups, tiled=True)]
  transfers between devices with their start and end apart: 57 -> 22, of which waited for: 19 -> 12; matrix products, arithmetic and copies ran while one was open for 12% -> 5% of each run, Pallas kernels for 12% -> 11%
where the time goes in v1:
time: 272 us; the launch traced here: 271 us
  waiting for transfers between devices  120 us (44%)
  blocking collectives  55.2 us (20%)
  starting transfers between devices  31.3 us (12%)
  Pallas kernels  28.6 us (11%)
  between operations  14.2 us (5%)
  other arithmetic  12.8 us (5%)
  local copies, waits for them, and re-layouts  7.53 us (3%)
    all_gather x2, waiting for transfers between devices, per_device(): lax.all_gather(line, 'seq', axis_index_groups=LINES, axis=0, tiled=False)  64.5 us
    ppermute x16, waiting for transfers between devices, from_z(): lax.ppermute(x, 'seq', [(seq_of(y, z + step, c), seq_of(y, z, c)) for y,...  44.1 us
    all_to_all x2, blocking collectives, scatter_gradient(): lax.all_to_all(total, 'seq', 0, 0, axis_index_groups=groups, tiled=True)  39.1 us
    ppermute x16, starting transfers between devices, from_z(): lax.ppermute(x, 'seq', [(seq_of(y, z + step, c), seq_of(y, z, c)) for y,...  30.7 us
    pallas_call x2, Pallas kernels, attend(): pl.pallas_call(functools.partial(attention_kernel, heads, last), grid_spe...  28.6 us
    all_gather x1, blocking collectives, normed_store(): whole = lax.all_gather(packed, 'tp', axis=1, tiled=True).astype(jnp.float32)  16.1 us
    reduce_scatter x2, waiting for transfers between devices, per_device(): lax.psum_scatter(att, 'seq', axis_index_groups=LINES, scatter_dimension=0...  9.93 us
  transfers between devices with their start and end apart: 22, of which 12 were waited for; matrix products, arithmetic and copies ran while one was open for 5% of the time, Pallas kernels for 11%

profile of v1, /device:TPU:2, one launch (start us, length us, event | category | flops | bytes accessed | tf_op | source)
XLA Modules:
  0.0 271.5 jit_solution(10268984537373165408)
XLA Ops:
  14.7 16.1 %all_gather.17 = bf16[272,1536]{0,1:T(8,128)(2,1)S(1)} all-gather(bf16[272,384]{0,1:T(8,128)(2,1)S(1)} %fusion.8), channel_id=1, replica_groups=mesh['seq'=64,'tp'=4] {'tp'}, dimensions={1}, use_global_device_ids=true | all-gather | bytes 1044480 | tf_op jit(solution)/shard_map/all_gather | solution.py:257
  36.4 4.0 %collective-permute-start = (bf16[256,1024]{1,0:T(8,128)(2,1)S(1)}, bf16[256,1024]{1,0:T(8,128)(2,1)S(1)}, u32[]{:S(2)}, u32[]{:S(2)}) collective-permute-start(bf16[256,1024]{1,0:T(8,128)(2,1)S(1)} %pad_maximum_fusion.3.refs_0_), channel_id=1, source_target_pairs={{8,0},{12,4},{16,8},{20,12},{24,16},{28,20},{32,24},{36,28},{40,32... | collective-permute-start | bytes 1572872 | tf_op jit(solution)/shard_map/keys_values/gather_1/z/ppermute | solution.py:45
  40.4 8.7 %collective-permute-done.1.refs_2_ = bf16[256,1024]{1,0:T(8,128)(2,1)S(1)} collective-permute-done((bf16[256,1024]{1,0:T(8,128)(2,1)S(1)}, bf16[256,1024]{1,0:T(8,128)(2,1)S(1)}, u32[]{:S(2)}, u32[]{:S(2)}) %collective-permute-start.1) | collective-permute-done | bytes 524320 | tf_op jit(solution)/shard_map/keys_values/gather_1/z/ppermute | solution.py:45
  49.1 3.3 %collective-permute-start.2 = (bf16[256,1024]{1,0:T(8,128)(2,1)S(1)}, bf16[256,1024]{1,0:T(8,128)(2,1)S(1)}, u32[]{:S(2)}, u32[]{:S(2)}) collective-permute-start(bf16[256,1024]{1,0:T(8,128)(2,1)S(1)} %collective-permute-done.refs_1_), channel_id=1, source_target_pairs={{8,0},{12,4},{16,8},{20,12},{24,16},{28,20},{32,24},{36,28},{40,32... | collective-permute-start | bytes 1572872 | tf_op jit(solution)/shard_map/keys_values/gather_2/z/ppermute | solution.py:45
  52.4 8.7 %collective-permute-done.3.refs_4_ = bf16[256,1024]{1,0:T(8,128)(2,1)S(1)} collective-permute-done((bf16[256,1024]{1,0:T(8,128)(2,1)S(1)}, bf16[256,1024]{1,0:T(8,128)(2,1)S(1)}, u32[]{:S(2)}, u32[]{:S(2)}) %collective-permute-start.3) | collective-permute-done | bytes 524320 | tf_op jit(solution)/shard_map/keys_values/gather_2/z/ppermute | solution.py:45
  61.1 3.3 %collective-permute-start.4 = (bf16[256,1024]{1,0:T(8,128)(2,1)S(1)}, bf16[256,1024]{1,0:T(8,128)(2,1)S(1)}, u32[]{:S(2)}, u32[]{:S(2)}) collective-permute-start(bf16[256,1024]{1,0:T(8,128)(2,1)S(1)} %collective-permute-done.2.refs_3_), channel_id=1, source_target_pairs={{8,0},{12,4},{16,8},{20,12},{24,16},{28,20},{32,24},{36,28},{40,32... | collective-permute-start | bytes 1572872 | tf_op jit(solution)/shard_map/keys_values/gather_3/z/ppermute | solution.py:45
  64.4 7.2 %collective-permute-done.5.refs_6_ = bf16[256,1024]{1,0:T(8,128)(2,1)} collective-permute-done((bf16[256,1024]{1,0:T(8,128)(2,1)S(1)}, bf16[256,1024]{1,0:T(8,128)(2,1)}, u32[]{:S(2)}, u32[]{:S(2)}) %collective-permute-start.5) | collective-permute-done | bytes 524320 | tf_op jit(solution)/shard_map/keys_values/gather_3/z/ppermute | solution.py:45
  74.0 3.5 %collective-permute-start.6 = (bf16[128,1024]{1,0:T(8,128)(2,1)}, bf16[128,1024]{1,0:T(8,128)(2,1)}, u32[]{:S(2)}, u32[]{:S(2)}) collective-permute-start(bf16[128,1024]{1,0:T(8,128)(2,1)} %slice.95), channel_id=1, source_target_pairs={{8,0},{12,4},{16,8},{20,12},{24,16},{28,20},{32,24},{36,28},{40,32... | collective-permute-start | bytes 786440 | tf_op jit(solution)/shard_map/keys_values/gather_far/z/ppermute | solution.py:45
  77.5 8.3 %all-gather.5.cloned.1.call-done = bf16[12416,512]{1,0:T(8,128)(2,1)} async-done(((bf16[1552,512]{1,0:T(8,128)(2,1)}), bf16[12416,512]{1,0:T(8,128)(2,1)}) %all-gather.5.cloned.1.call-update) | async-done | bytes 12714000 | tf_op jit(solution)/shard_map/spans/all_gather | solution.py:294
  87.9 14.1 %attend.2 = (bf16[8,768,512]{2,1,0:T(8,128)(2,1)}, f32[8,512,256]{2,1,0:T(8,128)}) custom-call(s32[1]{0:T(128)} %bitcast.3.number, s32[96]{0:T(128)S(1)} %get-tuple-element.35.listed, s32[96]{0:T(128)S(1)} %get-tuple-element.34.block, s32[192]{0:T(256)S(1)} %reshape.235.ids, bf16[8,1552,512]{2,1,0:T(8,128)(2,1)} %bitcast.35, ...), custom_call_target="tpu_custom_call" | custom-call | flops 1610612736 | bytes 29360128 | tf_op jit(solution)/shard_map/attend/pallas_call | solution.py:221
  102.3 56.2 %all-gather.7.cloned.1.call-done = bf16[12416,512]{1,0:T(8,128)(2,1)} async-done(((bf16[1552,512]{1,0:T(8,128)(2,1)}), bf16[12416,512]{1,0:T(8,128)(2,1)}) %all-gather.7.cloned.1.call-update) | async-done | bytes 12714000 | tf_op jit(solution)/shard_map/spans/all_gather | solution.py:294
  160.6 14.5 %attend.3 = (bf16[8,768,512]{2,1,0:T(8,128)(2,1)}, bf16[512,256]{1,0:T(8,128)(2,1)S(1)}, bf16[512,256]{1,0:T(8,128)(2,1)S(1)}, bf16[512,256]{1,0:T(8,128)(2,1)S(...) custom-call(s32[1]{0:T(128)} %bitcast.9.number, ...), custom_call_target="tpu_custom_call" | custom-call | flops 1610612736 | bytes 29360128 | tf_op jit(solution)/shard_map/attend/pallas_call | solution.py:221
  175.1 5.1 %collective-permute-start.13 = (bf16[256,256]{1,0:T(8,128)(2,1)S(1)}, bf16[256,256]{1,0:T(8,128)(2,1)S(1)}, u32[]{:S(2)}, u32[]{:S(2)}) collective-permute-start(bf16[256,256]{1,0:T(8,128)(2,1)S(1)} %get-tuple-element.27), channel_id=1, source_target_pairs={{8,0},{12,4},{16,8},{20,12},{24,16},{28,20},{32,24},{36,28},{40,32... | collective-permute-start | bytes 393224 | tf_op jit(solution)/shard_map/key_gradients/scatter_far/z/ppermute | solution.py:45
  182.8 3.7 %collective-permute-start.14 = (bf16[512,256]{1,0:T(8,128)(2,1)S(1)}, bf16[512,256]{1,0:T(8,128)(2,1)S(1)}, u32[]{:S(2)}, u32[]{:S(2)}) collective-permute-start(bf16[512,256]{1,0:T(8,128)(2,1)S(1)} %pad_maximum_fusion.5), channel_id=1, source_target_pairs={{8,0},{12,4},{16,8},{20,12},{24,16},{28,20},{32,24},{36,28},{40,32... | collective-permute-start | bytes 786440 | tf_op jit(solution)/shard_map/key_gradients/scatter_3/z/ppermute | solution.py:45
  186.7 4.9 %collective-permute-done.14 = bf16[512,256]{1,0:T(8,128)(2,1)S(1)} collective-permute-done((bf16[512,256]{1,0:T(8,128)(2,1)S(1)}, bf16[512,256]{1,0:T(8,128)(2,1)S(1)}, u32[]{:S(2)}, u32[]{:S(2)}) %collective-permute-start.14) | collective-permute-done | bytes 262176 | tf_op jit(solution)/shard_map/key_gradients/scatter_3/z/ppermute | solution.py:45
  191.6 3.1 %collective-permute-start.15 = (bf16[512,256]{1,0:T(8,128)(2,1)S(1)}, bf16[512,256]{1,0:T(8,128)(2,1)S(1)}, u32[]{:S(2)}, u32[]{:S(2)}) collective-permute-start(bf16[512,256]{1,0:T(8,128)(2,1)S(1)} %add_convert_fusion.2), channel_id=1, source_target_pairs={{8,0},{12,4},{16,8},{20,12},{24,16},{28,20},{32,24},{36,28},{40,32... | collective-permute-start | bytes 786440 | tf_op jit(solution)/shard_map/key_gradients/scatter_2/z/ppermute | solution.py:45
  194.9 4.9 %collective-permute-done.15 = bf16[512,256]{1,0:T(8,128)(2,1)S(1)} collective-permute-done((bf16[512,256]{1,0:T(8,128)(2,1)S(1)}, bf16[512,256]{1,0:T(8,128)(2,1)S(1)}, u32[]{:S(2)}, u32[]{:S(2)}) %collective-permute-start.15) | collective-permute-done | bytes 262176 | tf_op jit(solution)/shard_map/key_gradients/scatter_2/z/ppermute | solution.py:45
  199.9 2.6 collective-permute-start.16
  202.8 4.6 %collective-permute-done.16 = bf16[512,256]{1,0:T(8,128)(2,1)S(1)} collective-permute-done((bf16[512,256]{1,0:T(8,128)(2,1)S(1)}, bf16[512,256]{1,0:T(8,128)(2,1)S(1)}, u32[]{:S(2)}, u32[]{:S(2)}) %collective-permute-start.16) | collective-permute-done | bytes 262176 | tf_op jit(solution)/shard_map/key_gradients/scatter_1/z/ppermute | solution.py:45
  207.4 2.8 %collective-permute-done.12 = bf16[512,256]{1,0:T(8,128)(2,1)S(1)} collective-permute-done((bf16[512,256]{1,0:T(8,128)(2,1)S(1)}, bf16[512,256]{1,0:T(8,128)(2,1)S(1)}, u32[]{:S(2)}, u32[]{:S(2)}) %collective-permute-start.12) | collective-permute-done | bytes 262176 | tf_op jit(solution)/shard_map/key_gradients/scatter_1/z/ppermute | solution.py:45
  212.5 24.9 %all_to_all.10 = bf16[4,8,24,512]{3,2,1,0:T(8,128)(2,1)S(1)} all-to-all(bf16[4,8,24,512]{3,2,1,0:T(8,128)(2,1)S(1)} %bitcast.38), channel_id=1, replica_groups={{0,64,128,192},{4,68,132,196},{8,72,136,200},{12,76,140,204},{16,80,144..., dimensions={0} | all-to-all | bytes 1572864 | tf_op jit(solution)/shard_map/all_to_all | solution.py:273
  237.6 14.2 %all_to_all.11 = bf16[8,1,24,512]{3,2,1,0:T(8,128)(2,1)S(1)} all-to-all(bf16[8,1,24,512]{3,2,1,0:T(8,128)(2,1)S(1)} %bitcast.37), channel_id=1, replica_groups={{0,8,16,24,32,40,48,56},{4,12,20,28,36,44,52,60},{64,72,80,88,96,104,11..., dimensions={0} | all-to-all | bytes 393216 | tf_op jit(solution)/shard_map/all_to_all | solution.py:273
  252.4 9.9 %reduce-scatter.5.cloned.1.call-done = bf16[1,768,512]{2,1,0:T(8,128)(2,1)} async-done(((bf16[8,768,512]{2,1,0:T(8,128)(2,1)}), bf16[1,768,512]{2,1,0:T(8,128)(2,1)}) %reduce-scatter.5.cloned.1.call-update) | async-done | bytes 786448 | tf_op jit(solution)/shard_map/attended/reduce_scatter | solution.py:322
  262.3 2.6 pad_maximum_fusion.2
  (116 shorter events, 26.1 us)
Async XLA Ops:
  7.2 78.6 %all-gather.5.cloned.1.call-start = ((), (), s32[]{:S(2)}) async-start(), calls=%async_computation.6 | async-start | bytes 14303232 | tf_op jit(solution)/shard_map/spans/all_gather | solution.py:294
  12.2 146.3 %all-gather.7.cloned.1.call-start = ((), (), s32[]{:S(2)}) async-start(), calls=%async_computation.7 | async-start | bytes 14303232 | tf_op jit(solution)/shard_map/spans/all_gather | solution.py:294
  13.6 238.8 %reduce-scatter.3.cloned.1.call-start = ((), (), s32[]{:S(2)}) async-start(), calls=%async_computation.4 | async-start | bytes 7077888 | tf_op jit(solution)/shard_map/attended/reduce_scatter | solution.py:322
  34.6 14.5 %collective-permute-start.1 = (bf16[256,1024]{1,0:T(8,128)(2,1)S(1)}, bf16[256,1024]{1,0:T(8,128)(2,1)S(1)}, u32[]{:S(2)}, u32[]{:S(2)}) collective-permute-start(bf16[256,1024]{1,0:T(8,128)(2,1)S(1)} %pad_maximum_fusion.3.refs_0_), channel_id=1, source_target_pairs={{56,0},{60,4},{0,8},{4,12},{8,16},{12,20},{16,24},{20,28},{24,32},... | collective-permute-start | bytes 1572872 | tf_op jit(solution)/shard_map/keys_values/gather_1/z/ppermute | solution.py:45
  36.4 12.7 %collective-permute-start = (bf16[256,1024]{1,0:T(8,128)(2,1)S(1)}, bf16[256,1024]{1,0:T(8,128)(2,1)S(1)}, u32[]{:S(2)}, u32[]{:S(2)}) collective-permute-start(bf16[256,1024]{1,0:T(8,128)(2,1)S(1)} %pad_maximum_fusion.3.refs_0_), channel_id=1, source_target_pairs={{8,0},{12,4},{16,8},{20,12},{24,16},{28,20},{32,24},{36,28},{40,32... | collective-permute-start | bytes 1572872 | tf_op jit(solution)/shard_map/keys_values/gather_1/z/ppermute | solution.py:45
  49.1 52.9 %copy-start.3 = (bf16[256,1024]{1,0:T(8,128)(2,1)}, bf16[256,1024]{1,0:T(8,128)(2,1)S(1)}, u32[]{:S(2)}) copy-start(bf16[256,1024]{1,0:T(8,128)(2,1)S(1)} %collective-permute-done.1.refs_2_) | copy-start | bytes 1572868
  49.1 12.0 %collective-permute-start.3 = (bf16[256,1024]{1,0:T(8,128)(2,1)S(1)}, bf16[256,1024]{1,0:T(8,128)(2,1)S(1)}, u32[]{:S(2)}, u32[]{:S(2)}) collective-permute-start(bf16[256,1024]{1,0:T(8,128)(2,1)S(1)} %collective-permute-done.1.refs_2_), channel_id=1, source_target_pairs={{56,0},{60,4},{0,8},{4,12},{8,16},{12,20},{16,24},{20,28},{24,32},... | collective-permute-start | bytes 1572872 | tf_op jit(solution)/shard_map/keys_values/gather_2/z/ppermute | solution.py:45
  49.1 12.0 %collective-permute-start.2 = (bf16[256,1024]{1,0:T(8,128)(2,1)S(1)}, bf16[256,1024]{1,0:T(8,128)(2,1)S(1)}, u32[]{:S(2)}, u32[]{:S(2)}) collective-permute-start(bf16[256,1024]{1,0:T(8,128)(2,1)S(1)} %collective-permute-done.refs_1_), channel_id=1, source_target_pairs={{8,0},{12,4},{16,8},{20,12},{24,16},{28,20},{32,24},{36,28},{40,32... | collective-permute-start | bytes 1572872 | tf_op jit(solution)/shard_map/keys_values/gather_2/z/ppermute | solution.py:45
  61.1 41.0 %copy-start.4 = (bf16[256,1024]{1,0:T(8,128)(2,1)}, bf16[256,1024]{1,0:T(8,128)(2,1)S(1)}, u32[]{:S(2)}) copy-start(bf16[256,1024]{1,0:T(8,128)(2,1)S(1)} %collective-permute-done.3.refs_4_) | copy-start | bytes 1572868
  61.1 10.5 %collective-permute-start.5 = (bf16[256,1024]{1,0:T(8,128)(2,1)S(1)}, bf16[256,1024]{1,0:T(8,128)(2,1)}, u32[]{:S(2)}, u32[]{:S(2)}) collective-permute-start(bf16[256,1024]{1,0:T(8,128)(2,1)S(1)} %collective-permute-done.3.refs_4_), channel_id=1, source_target_pairs={{56,0},{60,4},{0,8},{4,12},{8,16},{12,20},{16,24},{20,28},{24,32},... | collective-permute-start | bytes 1572872 | tf_op jit(solution)/shard_map/keys_values/gather_3/z/ppermute | solution.py:45
  61.1 12.2 %collective-permute-start.4 = (bf16[256,1024]{1,0:T(8,128)(2,1)S(1)}, bf16[256,1024]{1,0:T(8,128)(2,1)S(1)}, u32[]{:S(2)}, u32[]{:S(2)}) collective-permute-start(bf16[256,1024]{1,0:T(8,128)(2,1)S(1)} %collective-permute-done.2.refs_3_), channel_id=1, source_target_pairs={{8,0},{12,4},{16,8},{20,12},{24,16},{28,20},{32,24},{36,28},{40,32... | collective-permute-start | bytes 1572872 | tf_op jit(solution)/shard_map/keys_values/gather_3/z/ppermute | solution.py:45
  73.3 14.6 %collective-permute-start.7 = (bf16[128,1024]{1,0:T(8,128)(2,1)}, bf16[128,1024]{1,0:T(8,128)(2,1)S(1)}, u32[]{:S(2)}, u32[]{:S(2)}) collective-permute-start(bf16[128,1024]{1,0:T(8,128)(2,1)} %slice.96), channel_id=1, source_target_pairs={{56,0},{60,4},{0,8},{4,12},{8,16},{12,20},{16,24},{20,28},{24,32},... | collective-permute-start | bytes 786440 | tf_op jit(solution)/shard_map/keys_values/gather_far/z/ppermute | solution.py:45
  74.0 13.8 %collective-permute-start.6 = (bf16[128,1024]{1,0:T(8,128)(2,1)}, bf16[128,1024]{1,0:T(8,128)(2,1)}, u32[]{:S(2)}, u32[]{:S(2)}) collective-permute-start(bf16[128,1024]{1,0:T(8,128)(2,1)} %slice.95), channel_id=1, source_target_pairs={{8,0},{12,4},{16,8},{20,12},{24,16},{28,20},{32,24},{36,28},{40,32... | collective-permute-start | bytes 786440 | tf_op jit(solution)/shard_map/keys_values/gather_far/z/ppermute | solution.py:45
  102.1 160.2 %reduce-scatter.5.cloned.1.call-start = ((), (), s32[]{:S(2)}) async-start(), calls=%async_computation.5 | async-start | bytes 7077888 | tf_op jit(solution)/shard_map/attended/reduce_scatter | solution.py:322
  175.1 7.6 %collective-permute-start.13 = (bf16[256,256]{1,0:T(8,128)(2,1)S(1)}, bf16[256,256]{1,0:T(8,128)(2,1)S(1)}, u32[]{:S(2)}, u32[]{:S(2)}) collective-permute-start(bf16[256,256]{1,0:T(8,128)(2,1)S(1)} %get-tuple-element.27), channel_id=1, source_target_pairs={{8,0},{12,4},{16,8},{20,12},{24,16},{28,20},{32,24},{36,28},{40,32... | collective-permute-start | bytes 393224 | tf_op jit(solution)/shard_map/key_gradients/scatter_far/z/ppermute | solution.py:45
  180.2 6.3 %collective-permute-start.9 = (bf16[256,256]{1,0:T(8,128)(2,1)S(1)}, bf16[256,256]{1,0:T(8,128)(2,1)S(1)}, u32[]{:S(2)}, u32[]{:S(2)}) collective-permute-start(bf16[256,256]{1,0:T(8,128)(2,1)S(1)} %get-tuple-element.23), channel_id=1, source_target_pairs={{56,0},{60,4},{0,8},{4,12},{8,16},{12,20},{16,24},{20,28},{24,32},... | collective-permute-start | bytes 393224 | tf_op jit(solution)/shard_map/key_gradients/scatter_far/z/ppermute | solution.py:45
  182.8 8.8 %collective-permute-start.14 = (bf16[512,256]{1,0:T(8,128)(2,1)S(1)}, bf16[512,256]{1,0:T(8,128)(2,1)S(1)}, u32[]{:S(2)}, u32[]{:S(2)}) collective-permute-start(bf16[512,256]{1,0:T(8,128)(2,1)S(1)} %pad_maximum_fusion.5), channel_id=1, source_target_pairs={{8,0},{12,4},{16,8},{20,12},{24,16},{28,20},{32,24},{36,28},{40,32... | collective-permute-start | bytes 786440 | tf_op jit(solution)/shard_map/key_gradients/scatter_3/z/ppermute | solution.py:45
  186.6 8.2 %collective-permute-start.10 = (bf16[512,256]{1,0:T(8,128)(2,1)S(1)}, bf16[512,256]{1,0:T(8,128)(2,1)S(1)}, u32[]{:S(2)}, u32[]{:S(2)}) collective-permute-start(bf16[512,256]{1,0:T(8,128)(2,1)S(1)} %pad_maximum_fusion.4), channel_id=1, source_target_pairs={{56,0},{60,4},{0,8},{4,12},{8,16},{12,20},{16,24},{20,28},{24,32},... | collective-permute-start | bytes 786440 | tf_op jit(solution)/shard_map/key_gradients/scatter_3/z/ppermute | solution.py:45
  191.6 8.1 %collective-permute-start.15 = (bf16[512,256]{1,0:T(8,128)(2,1)S(1)}, bf16[512,256]{1,0:T(8,128)(2,1)S(1)}, u32[]{:S(2)}, u32[]{:S(2)}) collective-permute-start(bf16[512,256]{1,0:T(8,128)(2,1)S(1)} %add_convert_fusion.2), channel_id=1, source_target_pairs={{8,0},{12,4},{16,8},{20,12},{24,16},{28,20},{32,24},{36,28},{40,32... | collective-permute-start | bytes 786440 | tf_op jit(solution)/shard_map/key_gradients/scatter_2/z/ppermute | solution.py:45
  194.8 7.7 %collective-permute-start.11 = (bf16[512,256]{1,0:T(8,128)(2,1)S(1)}, bf16[512,256]{1,0:T(8,128)(2,1)S(1)}, u32[]{:S(2)}, u32[]{:S(2)}) collective-permute-start(bf16[512,256]{1,0:T(8,128)(2,1)S(1)} %add_convert_fusion.4), channel_id=1, source_target_pairs={{56,0},{60,4},{0,8},{4,12},{8,16},{12,20},{16,24},{20,28},{24,32},... | collective-permute-start | bytes 786440 | tf_op jit(solution)/shard_map/key_gradients/scatter_2/z/ppermute | solution.py:45
  199.9 7.5 %collective-permute-start.16 = (bf16[512,256]{1,0:T(8,128)(2,1)S(1)}, bf16[512,256]{1,0:T(8,128)(2,1)S(1)}, u32[]{:S(2)}, u32[]{:S(2)}) collective-permute-start(bf16[512,256]{1,0:T(8,128)(2,1)S(1)} %add_convert_fusion.1), channel_id=1, source_target_pairs={{8,0},{12,4},{16,8},{20,12},{24,16},{28,20},{32,24},{36,28},{40,32... | collective-permute-start | bytes 786440 | tf_op jit(solution)/shard_map/key_gradients/scatter_1/z/ppermute | solution.py:45
  202.5 7.7 %collective-permute-start.12 = (bf16[512,256]{1,0:T(8,128)(2,1)S(1)}, bf16[512,256]{1,0:T(8,128)(2,1)S(1)}, u32[]{:S(2)}, u32[]{:S(2)}) collective-permute-start(bf16[512,256]{1,0:T(8,128)(2,1)S(1)} %add_convert_fusion.3), channel_id=1, source_target_pairs={{56,0},{60,4},{0,8},{4,12},{8,16},{12,20},{16,24},{20,28},{24,32},... | collective-permute-start | bytes 786440 | tf_op jit(solution)/shard_map/key_gradients/scatter_1/z/ppermute | solution.py:45
  202.7 7.7 %collective-permute-start.8 = (bf16[256,32,24]{0,2,1:T(8,128)(2,1)S(1)}, bf16[256,32,24]{0,2,1:T(8,128)(2,1)S(1)}, u32[]{:S(2)}, u32[]{:S(2)}) collective-permute-start(bf16[256,32,24]{0,2,1:T(8,128)(2,1)S(1)} %get-tuple-element.41), channel_id=1, source_target_pairs={{0,4},{4,0},{8,12},{12,8},{16,20},{20,16},{24,28},{28,24},{32,36},... | collective-permute-start | bytes 1179656 | tf_op jit(solution)/shard_map/swap/ppermute | solution.py:35
  210.3 1.6 collective-permute-start.17
  (9 other events, 129.7 us)
Sparse Core Ops, SparseCore 0:
  12.4 73.4 all-gather.4
  87.6 70.8 all-gather.6
  161.1 45.5 reduce-scatter.2
  209.1 53.1 reduce-scatter.4

commit v2 on v1

--- a/solution.py
+++ b/solution.py
@@ -310,7 +310,7 @@
     sums, attended = None, []
     for line in lines:
         if sums is not None:
-            line = after(line, sums[0])
+            line = after(line, (sums[0], att))
         meta = line[:, tokens : tokens + 3, : half // SPAN].astype(jnp.int32)
         owners, ids = meta[:, 0].reshape(-1), meta[:, 1:].transpose(0, 2, 1).reshape(-1)
         member = (owners % 2 == core) & (owners // (2 * N_Z) == here_y)
@@ -318,8 +318,15 @@
         with jax.named_scope("attend"):
             att, sums = attend(work, ids, line, half, kv, None if sums is None else sums[0])
         with jax.named_scope("attended"):
+            groups = LINES
+            if not attended:
+                att = att.reshape(N_Y, 2, half, local_width)
+                ours, theirs = (
+                    lax.dynamic_index_in_dim(att, which, 1, False) for which in (core, 1 - core)
+                )
+                att, groups = ours + swap(theirs), Y_GROUPS
             attended.append(
-                lax.psum_scatter(att, "seq", axis_index_groups=LINES, scatter_dimension=0, tiled=False)
+                lax.psum_scatter(att, "seq", axis_index_groups=groups, scatter_dimension=0, tiled=False)
             )
     with jax.named_scope("key_gradients"):
         grad_keys = ring_scatter(sums, from_z, N_Z)

time: 272 us -> 268 us (0.985)
  waiting for transfers between devices: 120 us -> 102 us
  starting transfers between devices: 31.3 us -> 37.9 us
  other arithmetic: 12.8 us -> 17.7 us
  local copies, waits for them, and re-layouts: 7.53 us -> 11.8 us
    all_gather x2, waiting for transfers between devices: 64.5 us -> 45 us  [per_device(): lax.all_gather(line, 'seq', axis_index_groups=LINES, axis=0, tiled=False)]
    ppermute x2 -> x3, waiting for transfers between devices: 1.51 us -> 7.71 us  [swap(): return lax.ppermute(x, 'seq', PAIR)]
    add x0 -> x1, other arithmetic: none -> 4.86 us  [per_device(): att, groups = (ours + swap(theirs), Y_GROUPS)]
    squeeze x0 -> x1, local copies, waits for them, and re-layouts: none -> 4.32 us  [per_device(): lax.dynamic_index_in_dim(att, which, 1, False)]
    ppermute x2 -> x3, starting transfers between devices: 0.19 us -> 3.79 us  [swap(): return lax.ppermute(x, 'seq', PAIR)]
    reduce_scatter x2, waiting for transfers between devices: 9.93 us -> 6.67 us  [per_device(): lax.psum_scatter(att, 'seq', axis_index_groups=groups, scatter_dimension=...]
    ppermute x16, starting transfers between devices: 30.7 us -> 33.9 us  [from_z(): lax.ppermute(x, 'seq', [(seq_of(y, z + step, c), seq_of(y, z, c)) for y,...]
  transfers between devices with their start and end apart: 22 -> 23, of which waited for: 12 -> 13; matrix products, arithmetic and copies ran while one was open for 5% -> 8% of each run, Pallas kernels for 11% -> 10%
where the time goes in v2:
time: 268 us; the launch traced here: 267 us
  waiting for transfers between devices  102 us (38%)
  blocking collectives  54.3 us (20%)
  starting transfers between devices  37.9 us (14%)
  Pallas kernels  27.7 us (10%)
  other arithmetic  17.7 us (7%)
  between operations  14.2 us (5%)
  local copies, waits for them, and re-layouts  11.8 us (4%)
    all_gather x2, waiting for transfers between devices, per_device(): lax.all_gather(line, 'seq', axis_index_groups=LINES, axis=0, tiled=False)  45 us
    ppermute x16, waiting for transfers between devices, from_z(): lax.ppermute(x, 'seq', [(seq_of(y, z + step, c), seq_of(y, z, c)) for y,...  42.4 us
    all_to_all x2, blocking collectives, scatter_gradient(): lax.all_to_all(total, 'seq', 0, 0, axis_index_groups=groups, tiled=True)  38.2 us
    ppermute x16, starting transfers between devices, from_z(): lax.ppermute(x, 'seq', [(seq_of(y, z + step, c), seq_of(y, z, c)) for y,...  33.9 us
    pallas_call x2, Pallas kernels, attend(): pl.pallas_call(functools.partial(attention_kernel, heads, last), grid_spe...  27.7 us
    all_gather x1, blocking collectives, normed_store(): whole = lax.all_gather(packed, 'tp', axis=1, tiled=True).astype(jnp.float32)  16.1 us
    ppermute x3, waiting for transfers between devices, swap(): return lax.ppermute(x, 'seq', PAIR)  7.71 us
    reduce_scatter x2, waiting for transfers between devices, per_device(): lax.psum_scatter(att, 'seq', axis_index_groups=groups, scatter_dimension=...  6.67 us
  transfers between devices with their start and end apart: 23, of which 13 were waited for; matrix products, arithmetic and copies ran while one was open for 8% of the time, Pallas kernels for 10%

profile of v2, /device:TPU:2, one launch (start us, length us, event | category | flops | bytes accessed | tf_op | source)
XLA Modules:
  0.0 267.2 jit_solution(5951364727528490424)
XLA Ops:
  14.7 16.1 %all_gather.17 = bf16[272,1536]{0,1:T(8,128)(2,1)S(1)} all-gather(bf16[272,384]{0,1:T(8,128)(2,1)S(1)} %fusion.8), channel_id=1, replica_groups=mesh['seq'=64,'tp'=4] {'tp'}, dimensions={1}, use_global_device_ids=true | all-gather | bytes 1044480 | tf_op jit(solution)/shard_map/all_gather | solution.py:257
  34.6 5.7 %collective-permute-start = (bf16[256,1024]{1,0:T(8,128)(2,1)S(1)}, bf16[256,1024]{1,0:T(8,128)(2,1)S(1)}, u32[]{:S(2)}, u32[]{:S(2)}) collective-permute-start(bf16[256,1024]{1,0:T(8,128)(2,1)S(1)} %pad_maximum_fusion.3.refs_0_), channel_id=1, source_target_pairs={{8,0},{12,4},{16,8},{20,12},{24,16},{28,20},{32,24},{36,28},{40,32... | collective-permute-start | bytes 1572872 | tf_op jit(solution)/shard_map/keys_values/gather_1/z/ppermute | solution.py:45
  40.3 8.3 %collective-permute-done.refs_1_ = bf16[256,1024]{1,0:T(8,128)(2,1)S(1)} collective-permute-done((bf16[256,1024]{1,0:T(8,128)(2,1)S(1)}, bf16[256,1024]{1,0:T(8,128)(2,1)S(1)}, u32[]{:S(2)}, u32[]{:S(2)}) %collective-permute-start) | collective-permute-done | bytes 524320 | tf_op jit(solution)/shard_map/keys_values/gather_1/z/ppermute | solution.py:45
  48.6 3.7 %collective-permute-start.2 = (bf16[256,1024]{1,0:T(8,128)(2,1)S(1)}, bf16[256,1024]{1,0:T(8,128)(2,1)S(1)}, u32[]{:S(2)}, u32[]{:S(2)}) collective-permute-start(bf16[256,1024]{1,0:T(8,128)(2,1)S(1)} %collective-permute-done.refs_1_), channel_id=1, source_target_pairs={{8,0},{12,4},{16,8},{20,12},{24,16},{28,20},{32,24},{36,28},{40,32... | collective-permute-start | bytes 1572872 | tf_op jit(solution)/shard_map/keys_values/gather_2/z/ppermute | solution.py:45
  52.3 8.3 %collective-permute-done.2.refs_3_ = bf16[256,1024]{1,0:T(8,128)(2,1)S(1)} collective-permute-done((bf16[256,1024]{1,0:T(8,128)(2,1)S(1)}, bf16[256,1024]{1,0:T(8,128)(2,1)S(1)}, u32[]{:S(2)}, u32[]{:S(2)}) %collective-permute-start.2) | collective-permute-done | bytes 524320 | tf_op jit(solution)/shard_map/keys_values/gather_2/z/ppermute | solution.py:45
  60.6 3.7 %collective-permute-start.4 = (bf16[256,1024]{1,0:T(8,128)(2,1)S(1)}, bf16[256,1024]{1,0:T(8,128)(2,1)S(1)}, u32[]{:S(2)}, u32[]{:S(2)}) collective-permute-start(bf16[256,1024]{1,0:T(8,128)(2,1)S(1)} %collective-permute-done.2.refs_3_), channel_id=1, source_target_pairs={{8,0},{12,4},{16,8},{20,12},{24,16},{28,20},{32,24},{36,28},{40,32... | collective-permute-start | bytes 1572872 | tf_op jit(solution)/shard_map/keys_values/gather_3/z/ppermute | solution.py:45
  64.4 7.7 %collective-permute-done.4.refs_5_ = bf16[256,1024]{1,0:T(8,128)(2,1)S(1)} collective-permute-done((bf16[256,1024]{1,0:T(8,128)(2,1)S(1)}, bf16[256,1024]{1,0:T(8,128)(2,1)S(1)}, u32[]{:S(2)}, u32[]{:S(2)}) %collective-permute-start.4) | collective-permute-done | bytes 524320 | tf_op jit(solution)/shard_map/keys_values/gather_3/z/ppermute | solution.py:45
  72.9 3.7 %collective-permute-start.6 = (bf16[128,1024]{1,0:T(8,128)(2,1)}, bf16[128,1024]{1,0:T(8,128)(2,1)S(1)}, u32[]{:S(2)}, u32[]{:S(2)}) collective-permute-start(bf16[128,1024]{1,0:T(8,128)(2,1)} %slice.95), channel_id=1, source_target_pairs={{8,0},{12,4},{16,8},{20,12},{24,16},{28,20},{32,24},{36,28},{40,32... | collective-permute-start | bytes 786440 | tf_op jit(solution)/shard_map/keys_values/gather_far/z/ppermute | solution.py:45
  78.2 7.6 %all-gather.5.cloned.1.call-done = bf16[12416,512]{1,0:T(8,128)(2,1)} async-done(((bf16[1552,512]{1,0:T(8,128)(2,1)}), bf16[12416,512]{1,0:T(8,128)(2,1)}) %all-gather.5.cloned.1.call-update) | async-done | bytes 12714000 | tf_op jit(solution)/shard_map/spans/all_gather | solution.py:294
  87.9 14.1 %attend.2 = (bf16[8,768,512]{2,1,0:T(8,128)(2,1)}, f32[8,512,256]{2,1,0:T(8,128)}) custom-call(s32[1]{0:T(128)} %bitcast.3.number, s32[96]{0:T(128)S(1)} %get-tuple-element.35.listed, s32[96]{0:T(128)S(1)} %get-tuple-element.34.block, s32[192]{0:T(256)S(1)} %reshape.238.ids, bf16[8,1552,512]{2,1,0:T(8,128)(2,1)} %bitcast.44, ...), custom_call_target="tpu_custom_call" | custom-call | flops 1610612736 | bytes 29360128 | tf_op jit(solution)/shard_map/attend/pallas_call | solution.py:221
  102.1 4.3 %dynamic-slice_bitcast_fusion = bf16[4,768,512]{2,1,0:T(8,128)(2,1)} fusion(bf16[4,2,768,512]{3,2,1,0:T(8,128)(2,1)} %bitcast.46, s32[]{:T(128)S(6)} %select_n.176), kind=kLoop, calls=%fused_computation.1 | loop fusion | bytes 6291460 | tf_op jit(solution)/shard_map/attended/jit(dynamic_index_in_dim)/squeeze | solution.py:325
  106.4 3.6 %collective-permute-start.8 = (bf16[4,768,512]{2,1,0:T(8,128)(2,1)}, bf16[4,768,512]{2,1,0:T(8,128)(2,1)}, u32[]{:S(2)}, u32[]{:S(2)}) collective-permute-start(bf16[4,768,512]{2,1,0:T(8,128)(2,1)} %dynamic-slice_bitcast_fusion), channel_id=1, source_target_pairs={{0,4},{4,0},{8,12},{12,8},{16,20},{20,16},{24,28},{28,24},{32,36},... | collective-permute-start | bytes 9437192 | tf_op jit(solution)/shard_map/attended/swap/ppermute | solution.py:35
  110.0 6.2 %collective-permute-done.8 = bf16[4,768,512]{2,1,0:T(8,128)(2,1)} collective-permute-done((bf16[4,768,512]{2,1,0:T(8,128)(2,1)}, bf16[4,768,512]{2,1,0:T(8,128)(2,1)}, u32[]{:S(2)}, u32[]{:S(2)}) %collective-permute-start.8) | collective-permute-done | bytes 3145760 | tf_op jit(solution)/shard_map/attended/swap/ppermute | solution.py:35
  116.2 4.9 %bitcast_add_fusion = bf16[4,768,512]{2,1,0:T(8,128)(2,1)} fusion(bf16[4,768,512]{2,1,0:T(8,128)(2,1)} %collective-permute-done.8, bf16[4,2,768,512]{3,2,1,0:T(8,128)(2,1)} %bitcast.47, s32[]{:T(128)S(6)} %select_n.175), kind=kLoop, calls=%fused_computation | loop fusion | flops 1572864 | bytes 9437188 | tf_op jit(solution)/shard_map/attended/add | solution.py:327
  121.1 37.4 %all-gather.7.cloned.1.call-done = bf16[12416,512]{1,0:T(8,128)(2,1)} async-done(((bf16[1552,512]{1,0:T(8,128)(2,1)}), bf16[12416,512]{1,0:T(8,128)(2,1)}) %all-gather.7.cloned.1.call-update) | async-done | bytes 12714000 | tf_op jit(solution)/shard_map/spans/all_gather | solution.py:294
  160.6 13.6 %attend.3 = (bf16[8,768,512]{2,1,0:T(8,128)(2,1)}, bf16[512,256]{1,0:T(8,128)(2,1)S(1)}, bf16[512,256]{1,0:T(8,128)(2,1)S(1)}, bf16[512,256]{1,0:T(8,128)(2,1)S(...) custom-call(s32[1]{0:T(128)} %bitcast.12.number, ...), custom_call_target="tpu_custom_call" | custom-call | flops 1610612736 | bytes 29360128 | tf_op jit(solution)/shard_map/attend/pallas_call | solution.py:221
  174.2 5.1 %collective-permute-start.10 = (bf16[256,256]{1,0:T(8,128)(2,1)S(1)}, bf16[256,256]{1,0:T(8,128)(2,1)S(1)}, u32[]{:S(2)}, u32[]{:S(2)}) collective-permute-start(bf16[256,256]{1,0:T(8,128)(2,1)S(1)} %get-tuple-element.23), channel_id=1, source_target_pairs={{56,0},{60,4},{0,8},{4,12},{8,16},{12,20},{16,24},{20,28},{24,32},... | collective-permute-start | bytes 393224 | tf_op jit(solution)/shard_map/key_gradients/scatter_far/z/ppermute | solution.py:45
  187.6 4.9 %collective-permute-done.11 = bf16[512,256]{1,0:T(8,128)(2,1)S(1)} collective-permute-done((bf16[512,256]{1,0:T(8,128)(2,1)S(1)}, bf16[512,256]{1,0:T(8,128)(2,1)S(1)}, u32[]{:S(2)}, u32[]{:S(2)}) %collective-permute-start.11) | collective-permute-done | bytes 262176 | tf_op jit(solution)/shard_map/key_gradients/scatter_3/z/ppermute | solution.py:45
  192.7 3.3 %collective-permute-start.16 = (bf16[512,256]{1,0:T(8,128)(2,1)S(1)}, bf16[512,256]{1,0:T(8,128)(2,1)S(1)}, u32[]{:S(2)}, u32[]{:S(2)}) collective-permute-start(bf16[512,256]{1,0:T(8,128)(2,1)S(1)} %add_convert_fusion.2), channel_id=1, source_target_pairs={{8,0},{12,4},{16,8},{20,12},{24,16},{28,20},{32,24},{36,28},{40,32... | collective-permute-start | bytes 786440 | tf_op jit(solution)/shard_map/key_gradients/scatter_2/z/ppermute | solution.py:45
  196.0 4.2 %collective-permute-done.12 = bf16[512,256]{1,0:T(8,128)(2,1)S(1)} collective-permute-done((bf16[512,256]{1,0:T(8,128)(2,1)S(1)}, bf16[512,256]{1,0:T(8,128)(2,1)S(1)}, u32[]{:S(2)}, u32[]{:S(2)}) %collective-permute-start.12) | collective-permute-done | bytes 262176 | tf_op jit(solution)/shard_map/key_gradients/scatter_2/z/ppermute | solution.py:45
  203.9 4.0 %collective-permute-done.13 = bf16[512,256]{1,0:T(8,128)(2,1)S(1)} collective-permute-done((bf16[512,256]{1,0:T(8,128)(2,1)S(1)}, bf16[512,256]{1,0:T(8,128)(2,1)S(1)}, u32[]{:S(2)}, u32[]{:S(2)}) %collective-permute-start.13) | collective-permute-done | bytes 262176 | tf_op jit(solution)/shard_map/key_gradients/scatter_1/z/ppermute | solution.py:45
  212.4 23.1 %all_to_all.10 = bf16[4,8,24,512]{3,2,1,0:T(8,128)(2,1)S(1)} all-to-all(bf16[4,8,24,512]{3,2,1,0:T(8,128)(2,1)S(1)} %bitcast.49), channel_id=1, replica_groups={{0,64,128,192},{4,68,132,196},{8,72,136,200},{12,76,140,204},{16,80,144..., dimensions={0} | all-to-all | bytes 1572864 | tf_op jit(solution)/shard_map/all_to_all | solution.py:273
  235.6 15.1 %all_to_all.11 = bf16[8,1,24,512]{3,2,1,0:T(8,128)(2,1)S(1)} all-to-all(bf16[8,1,24,512]{3,2,1,0:T(8,128)(2,1)S(1)} %bitcast.48), channel_id=1, replica_groups={{0,8,16,24,32,40,48,56},{4,12,20,28,36,44,52,60},{64,72,80,88,96,104,11..., dimensions={0} | all-to-all | bytes 393216 | tf_op jit(solution)/shard_map/all_to_all | solution.py:273
  251.4 6.7 %reduce-scatter.5.cloned.1.call-done = bf16[1,768,512]{2,1,0:T(8,128)(2,1)} async-done(((bf16[8,768,512]{2,1,0:T(8,128)(2,1)}), bf16[1,768,512]{2,1,0:T(8,128)(2,1)}) %reduce-scatter.5.cloned.1.call-update) | async-done | bytes 786448 | tf_op jit(solution)/shard_map/attended/reduce_scatter | solution.py:329
  (120 shorter events, 37.8 us)
Async XLA Ops:
  7.2 78.6 %all-gather.5.cloned.1.call-start = ((), (), s32[]{:S(2)}) async-start(), calls=%async_computation.6 | async-start | bytes 14303232 | tf_op jit(solution)/shard_map/spans/all_gather | solution.py:294
  12.2 146.3 %all-gather.7.cloned.1.call-start = ((), (), s32[]{:S(2)}) async-start(), calls=%async_computation.7 | async-start | bytes 14303232 | tf_op jit(solution)/shard_map/spans/all_gather | solution.py:294
  13.6 237.8 %reduce-scatter.3.cloned.1.call-start = ((), (), s32[]{:S(2)}) async-start(), calls=%async_computation.4 | async-start | bytes 3932160 | tf_op jit(solution)/shard_map/attended/reduce_scatter | solution.py:329
  34.6 14.0 %collective-permute-start = (bf16[256,1024]{1,0:T(8,128)(2,1)S(1)}, bf16[256,1024]{1,0:T(8,128)(2,1)S(1)}, u32[]{:S(2)}, u32[]{:S(2)}) collective-permute-start(bf16[256,1024]{1,0:T(8,128)(2,1)S(1)} %pad_maximum_fusion.3.refs_0_), channel_id=1, source_target_pairs={{8,0},{12,4},{16,8},{20,12},{24,16},{28,20},{32,24},{36,28},{40,32... | collective-permute-start | bytes 1572872 | tf_op jit(solution)/shard_map/keys_values/gather_1/z/ppermute | solution.py:45
  40.3 12.0 %collective-permute-start.1 = (bf16[256,1024]{1,0:T(8,128)(2,1)S(1)}, bf16[256,1024]{1,0:T(8,128)(2,1)S(1)}, u32[]{:S(2)}, u32[]{:S(2)}) collective-permute-start(bf16[256,1024]{1,0:T(8,128)(2,1)S(1)} %pad_maximum_fusion.3.refs_0_), channel_id=1, source_target_pairs={{56,0},{60,4},{0,8},{4,12},{8,16},{12,20},{16,24},{20,28},{24,32},... | collective-permute-start | bytes 1572872 | tf_op jit(solution)/shard_map/keys_values/gather_1/z/ppermute | solution.py:45
  48.6 12.0 %collective-permute-start.2 = (bf16[256,1024]{1,0:T(8,128)(2,1)S(1)}, bf16[256,1024]{1,0:T(8,128)(2,1)S(1)}, u32[]{:S(2)}, u32[]{:S(2)}) collective-permute-start(bf16[256,1024]{1,0:T(8,128)(2,1)S(1)} %collective-permute-done.refs_1_), channel_id=1, source_target_pairs={{8,0},{12,4},{16,8},{20,12},{24,16},{28,20},{32,24},{36,28},{40,32... | collective-permute-start | bytes 1572872 | tf_op jit(solution)/shard_map/keys_values/gather_2/z/ppermute | solution.py:45
  52.3 49.7 %copy-start.3 = (bf16[256,1024]{1,0:T(8,128)(2,1)}, bf16[256,1024]{1,0:T(8,128)(2,1)S(1)}, u32[]{:S(2)}) copy-start(bf16[256,1024]{1,0:T(8,128)(2,1)S(1)} %collective-permute-done.1.refs_2_) | copy-start | bytes 1572868
  52.3 12.0 %collective-permute-start.3 = (bf16[256,1024]{1,0:T(8,128)(2,1)S(1)}, bf16[256,1024]{1,0:T(8,128)(2,1)S(1)}, u32[]{:S(2)}, u32[]{:S(2)}) collective-permute-start(bf16[256,1024]{1,0:T(8,128)(2,1)S(1)} %collective-permute-done.1.refs_2_), channel_id=1, source_target_pairs={{56,0},{60,4},{0,8},{4,12},{8,16},{12,20},{16,24},{20,28},{24,32},... | collective-permute-start | bytes 1572872 | tf_op jit(solution)/shard_map/keys_values/gather_2/z/ppermute | solution.py:45
  60.6 11.5 %collective-permute-start.4 = (bf16[256,1024]{1,0:T(8,128)(2,1)S(1)}, bf16[256,1024]{1,0:T(8,128)(2,1)S(1)}, u32[]{:S(2)}, u32[]{:S(2)}) collective-permute-start(bf16[256,1024]{1,0:T(8,128)(2,1)S(1)} %collective-permute-done.2.refs_3_), channel_id=1, source_target_pairs={{8,0},{12,4},{16,8},{20,12},{24,16},{28,20},{32,24},{36,28},{40,32... | collective-permute-start | bytes 1572872 | tf_op jit(solution)/shard_map/keys_values/gather_3/z/ppermute | solution.py:45
  64.3 12.2 %collective-permute-start.5 = (bf16[256,1024]{1,0:T(8,128)(2,1)S(1)}, bf16[256,1024]{1,0:T(8,128)(2,1)}, u32[]{:S(2)}, u32[]{:S(2)}) collective-permute-start(bf16[256,1024]{1,0:T(8,128)(2,1)S(1)} %collective-permute-done.3.refs_4_), channel_id=1, source_target_pairs={{56,0},{60,4},{0,8},{4,12},{8,16},{12,20},{16,24},{20,28},{24,32},... | collective-permute-start | bytes 1572872 | tf_op jit(solution)/shard_map/keys_values/gather_3/z/ppermute | solution.py:45
  72.9 15.0 %collective-permute-start.6 = (bf16[128,1024]{1,0:T(8,128)(2,1)}, bf16[128,1024]{1,0:T(8,128)(2,1)S(1)}, u32[]{:S(2)}, u32[]{:S(2)}) collective-permute-start(bf16[128,1024]{1,0:T(8,128)(2,1)} %slice.95), channel_id=1, source_target_pairs={{8,0},{12,4},{16,8},{20,12},{24,16},{28,20},{32,24},{36,28},{40,32... | collective-permute-start | bytes 786440 | tf_op jit(solution)/shard_map/keys_values/gather_far/z/ppermute | solution.py:45
  78.2 9.7 %collective-permute-start.7 = (bf16[128,1024]{1,0:T(8,128)(2,1)}, bf16[128,1024]{1,0:T(8,128)(2,1)}, u32[]{:S(2)}, u32[]{:S(2)}) collective-permute-start(bf16[128,1024]{1,0:T(8,128)(2,1)} %slice.96), channel_id=1, source_target_pairs={{56,0},{60,4},{0,8},{4,12},{8,16},{12,20},{16,24},{20,28},{24,32},... | collective-permute-start | bytes 786440 | tf_op jit(solution)/shard_map/keys_values/gather_far/z/ppermute | solution.py:45
  106.4 9.8 %collective-permute-start.8 = (bf16[4,768,512]{2,1,0:T(8,128)(2,1)}, bf16[4,768,512]{2,1,0:T(8,128)(2,1)}, u32[]{:S(2)}, u32[]{:S(2)}) collective-permute-start(bf16[4,768,512]{2,1,0:T(8,128)(2,1)} %dynamic-slice_bitcast_fusion), channel_id=1, source_target_pairs={{0,4},{4,0},{8,12},{12,8},{16,20},{20,16},{24,28},{28,24},{32,36},... | collective-permute-start | bytes 9437192 | tf_op jit(solution)/shard_map/attended/swap/ppermute | solution.py:35
  121.1 137.0 %reduce-scatter.5.cloned.1.call-start = ((), (), s32[]{:S(2)}) async-start(), calls=%async_computation.5 | async-start | bytes 7077888 | tf_op jit(solution)/shard_map/attended/reduce_scatter | solution.py:329
  174.2 9.9 %collective-permute-start.10 = (bf16[256,256]{1,0:T(8,128)(2,1)S(1)}, bf16[256,256]{1,0:T(8,128)(2,1)S(1)}, u32[]{:S(2)}, u32[]{:S(2)}) collective-permute-start(bf16[256,256]{1,0:T(8,128)(2,1)S(1)} %get-tuple-element.23), channel_id=1, source_target_pairs={{56,0},{60,4},{0,8},{4,12},{8,16},{12,20},{16,24},{20,28},{24,32},... | collective-permute-start | bytes 393224 | tf_op jit(solution)/shard_map/key_gradients/scatter_far/z/ppermute | solution.py:45
  179.3 5.1 %collective-permute-start.14 = (bf16[256,256]{1,0:T(8,128)(2,1)S(1)}, bf16[256,256]{1,0:T(8,128)(2,1)S(1)}, u32[]{:S(2)}, u32[]{:S(2)}) collective-permute-start(bf16[256,256]{1,0:T(8,128)(2,1)S(1)} %get-tuple-element.27), channel_id=1, source_target_pairs={{8,0},{12,4},{16,8},{20,12},{24,16},{28,20},{32,24},{36,28},{40,32... | collective-permute-start | bytes 393224 | tf_op jit(solution)/shard_map/key_gradients/scatter_far/z/ppermute | solution.py:45
  184.2 8.3 %collective-permute-start.11 = (bf16[512,256]{1,0:T(8,128)(2,1)S(1)}, bf16[512,256]{1,0:T(8,128)(2,1)S(1)}, u32[]{:S(2)}, u32[]{:S(2)}) collective-permute-start(bf16[512,256]{1,0:T(8,128)(2,1)S(1)} %pad_maximum_fusion.4), channel_id=1, source_target_pairs={{56,0},{60,4},{0,8},{4,12},{8,16},{12,20},{16,24},{20,28},{24,32},... | collective-permute-start | bytes 786440 | tf_op jit(solution)/shard_map/key_gradients/scatter_3/z/ppermute | solution.py:45
  184.5 8.2 %collective-permute-start.15 = (bf16[512,256]{1,0:T(8,128)(2,1)S(1)}, bf16[512,256]{1,0:T(8,128)(2,1)S(1)}, u32[]{:S(2)}, u32[]{:S(2)}) collective-permute-start(bf16[512,256]{1,0:T(8,128)(2,1)S(1)} %pad_maximum_fusion.5), channel_id=1, source_target_pairs={{8,0},{12,4},{16,8},{20,12},{24,16},{28,20},{32,24},{36,28},{40,32... | collective-permute-start | bytes 786440 | tf_op jit(solution)/shard_map/key_gradients/scatter_3/z/ppermute | solution.py:45
  192.6 7.7 %collective-permute-start.12 = (bf16[512,256]{1,0:T(8,128)(2,1)S(1)}, bf16[512,256]{1,0:T(8,128)(2,1)S(1)}, u32[]{:S(2)}, u32[]{:S(2)}) collective-permute-start(bf16[512,256]{1,0:T(8,128)(2,1)S(1)} %add_convert_fusion.4), channel_id=1, source_target_pairs={{56,0},{60,4},{0,8},{4,12},{8,16},{12,20},{16,24},{20,28},{24,32},... | collective-permute-start | bytes 786440 | tf_op jit(solution)/shard_map/key_gradients/scatter_2/z/ppermute | solution.py:45
  192.7 7.7 %collective-permute-start.16 = (bf16[512,256]{1,0:T(8,128)(2,1)S(1)}, bf16[512,256]{1,0:T(8,128)(2,1)S(1)}, u32[]{:S(2)}, u32[]{:S(2)}) collective-permute-start(bf16[512,256]{1,0:T(8,128)(2,1)S(1)} %add_convert_fusion.2), channel_id=1, source_target_pairs={{8,0},{12,4},{16,8},{20,12},{24,16},{28,20},{32,24},{36,28},{40,32... | collective-permute-start | bytes 786440 | tf_op jit(solution)/shard_map/key_gradients/scatter_2/z/ppermute | solution.py:45
  200.3 7.7 %collective-permute-start.13 = (bf16[512,256]{1,0:T(8,128)(2,1)S(1)}, bf16[512,256]{1,0:T(8,128)(2,1)S(1)}, u32[]{:S(2)}, u32[]{:S(2)}) collective-permute-start(bf16[512,256]{1,0:T(8,128)(2,1)S(1)} %add_convert_fusion.3), channel_id=1, source_target_pairs={{56,0},{60,4},{0,8},{4,12},{8,16},{12,20},{16,24},{20,28},{24,32},... | collective-permute-start | bytes 786440 | tf_op jit(solution)/shard_map/key_gradients/scatter_1/z/ppermute | solution.py:45
  200.5 9.6 %collective-permute-start.17 = (bf16[512,256]{1,0:T(8,128)(2,1)S(1)}, bf16[512,256]{1,0:T(8,128)(2,1)S(1)}, u32[]{:S(2)}, u32[]{:S(2)}) collective-permute-start(bf16[512,256]{1,0:T(8,128)(2,1)S(1)} %add_convert_fusion.1), channel_id=1, source_target_pairs={{8,0},{12,4},{16,8},{20,12},{24,16},{28,20},{32,24},{36,28},{40,32... | collective-permute-start | bytes 786440 | tf_op jit(solution)/shard_map/key_gradients/scatter_1/z/ppermute | solution.py:45
  203.8 6.4 %collective-permute-start.9 = (bf16[256,32,24]{0,2,1:T(8,128)(2,1)S(1)}, bf16[256,32,24]{0,2,1:T(8,128)(2,1)S(1)}, u32[]{:S(2)}, u32[]{:S(2)}) collective-permute-start(bf16[256,32,24]{0,2,1:T(8,128)(2,1)S(1)} %get-tuple-element.41), channel_id=1, source_target_pairs={{0,4},{4,0},{8,12},{12,8},{16,20},{20,16},{24,28},{28,24},{32,36},... | collective-permute-start | bytes 1179656 | tf_op jit(solution)/shard_map/swap/ppermute | solution.py:35
  210.2 1.6 collective-permute-start.18
  (10 other events, 169.1 us)
Sparse Core Ops, SparseCore 0:
  12.4 73.4 all-gather.4
  87.6 70.8 all-gather.6
  161.1 41.2 reduce-scatter.2
  204.8 53.2 reduce-scatter.4

commit v3 on v1

--- a/solution.py
+++ b/solution.py
@@ -310,7 +310,7 @@
     sums, attended = None, []
     for line in lines:
         if sums is not None:
-            line = after(line, sums[0])
+            line = after(line, (sums[0], att))
         meta = line[:, tokens : tokens + 3, : half // SPAN].astype(jnp.int32)
         owners, ids = meta[:, 0].reshape(-1), meta[:, 1:].transpose(0, 2, 1).reshape(-1)
         member = (owners % 2 == core) & (owners // (2 * N_Z) == here_y)
@@ -318,8 +318,15 @@
         with jax.named_scope("attend"):
             att, sums = attend(work, ids, line, half, kv, None if sums is None else sums[0])
         with jax.named_scope("attended"):
+            att = att.reshape(N_Y, 2, -1, local_width)
+            ours, theirs = (
+                lax.dynamic_index_in_dim(att, which, 1, False) for which in (core, 1 - core)
+            )
+            att = ours + swap(theirs)
             attended.append(
-                lax.psum_scatter(att, "seq", axis_index_groups=LINES, scatter_dimension=0, tiled=False)
+                lax.psum_scatter(
+                    att, "seq", axis_index_groups=Y_GROUPS, scatter_dimension=0, tiled=False
+                )
             )
     with jax.named_scope("key_gradients"):
         grad_keys = ring_scatter(sums, from_z, N_Z)

time: 272 us -> 277 us (1.018)
  waiting for transfers between devices: 120 us -> 103 us
  other arithmetic: 12.8 us -> 19.9 us
  local copies, waits for them, and re-layouts: 7.53 us -> 12.7 us
  blocking collectives: 55.2 us -> 60.1 us
  Pallas kernels: 28.6 us -> 32.9 us
    all_gather x2, waiting for transfers between devices: 64.5 us -> 47.6 us  [per_device(): lax.all_gather(line, 'seq', axis_index_groups=LINES, axis=0, tiled=False)]
    ppermute x2 -> x4, waiting for transfers between devices: 1.51 us -> 12.9 us  [swap(): return lax.ppermute(x, 'seq', PAIR)]
    reduce_scatter x2, waiting for transfers between devices: 9.93 us -> 0.01 us  [per_device(): lax.psum_scatter(att, 'seq', axis_index_groups=Y_GROUPS, scatter_dimensio...]
    add x0 -> x2, other arithmetic: none -> 7.06 us  [per_device(): att = ours + swap(theirs)]
    squeeze x0 -> x2, local copies, waits for them, and re-layouts: none -> 6.01 us  [per_device(): lax.dynamic_index_in_dim(att, which, 1, False)]
    all_to_all x2, blocking collectives: 39.1 us -> 44 us  [scatter_gradient(): lax.all_to_all(total, 'seq', 0, 0, axis_index_groups=groups, tiled=True)]
    pallas_call x2, Pallas kernels: 28.6 us -> 32.9 us  [attend(): pl.pallas_call(functools.partial(attention_kernel, heads, last), grid_spe...]
  transfers between devices with their start and end apart: 22 -> 24, of which waited for: 12 -> 12; matrix products, arithmetic and copies ran while one was open for 5% -> 9% of each run, Pallas kernels for 11% -> 12%
where the time goes in v3:
time: 277 us
  waiting for transfers between devices  103 us (37%)
  blocking collectives  60.1 us (22%)
  Pallas kernels  32.9 us (12%)
  starting transfers between devices  31.9 us (12%)
  other arithmetic  19.9 us (7%)
  between operations  14.3 us (5%)
  local copies, waits for them, and re-layouts  12.7 us (5%)
    all_gather x2, waiting for transfers between devices, per_device(): lax.all_gather(line, 'seq', axis_index_groups=LINES, axis=0, tiled=False)  47.6 us
    all_to_all x2, blocking collectives, scatter_gradient(): lax.all_to_all(total, 'seq', 0, 0, axis_index_groups=groups, tiled=True)  44 us
    ppermute x16, waiting for transfers between devices, from_z(): lax.ppermute(x, 'seq', [(seq_of(y, z + step, c), seq_of(y, z, c)) for y,...  42.5 us
    pallas_call x2, Pallas kernels, attend(): pl.pallas_call(functools.partial(attention_kernel, heads, last), grid_spe...  32.9 us
    ppermute x16, starting transfers between devices, from_z(): lax.ppermute(x, 'seq', [(seq_of(y, z + step, c), seq_of(y, z, c)) for y,...  31.2 us
    all_gather x1, blocking collectives, normed_store(): whole = lax.all_gather(packed, 'tp', axis=1, tiled=True).astype(jnp.float32)  16.1 us
    ppermute x4, waiting for transfers between devices, swap(): return lax.ppermute(x, 'seq', PAIR)  12.9 us
    add x2, other arithmetic, per_device(): att = ours + swap(theirs)  7.06 us
  transfers between devices with their start and end apart: 24, of which 12 were waited for; matrix products, arithmetic and copies ran while one was open for 9% of the time, Pallas kernels for 12%

profile of v3, /device:TPU:2, one launch (start us, length us, event | category | flops | bytes accessed | tf_op | source)
XLA Modules:
  0.0 276.6 jit_solution(4449462633121574558)
XLA Ops:
  14.1 16.1 %all_gather.17 = bf16[272,1536]{0,1:T(8,128)(2,1)S(1)} all-gather(bf16[272,384]{0,1:T(8,128)(2,1)S(1)} %fusion.8), channel_id=1, replica_groups=mesh['seq'=64,'tp'=4] {'tp'}, dimensions={1}, use_global_device_ids=true | all-gather | bytes 1044480 | tf_op jit(solution)/shard_map/all_gather | solution.py:257
  33.8 5.6 %collective-permute-start = (bf16[256,1024]{1,0:T(8,128)(2,1)S(1)}, bf16[256,1024]{1,0:T(8,128)(2,1)S(1)}, u32[]{:S(2)}, u32[]{:S(2)}) collective-permute-start(bf16[256,1024]{1,0:T(8,128)(2,1)S(1)} %pad_maximum_fusion.3.refs_0_), channel_id=1, source_target_pairs={{8,0},{12,4},{16,8},{20,12},{24,16},{28,20},{32,24},{36,28},{40,32... | collective-permute-start | bytes 1572872 | tf_op jit(solution)/shard_map/keys_values/gather_1/z/ppermute | solution.py:45
  39.5 8.3 %collective-permute-done.refs_1_ = bf16[256,1024]{1,0:T(8,128)(2,1)S(1)} collective-permute-done((bf16[256,1024]{1,0:T(8,128)(2,1)S(1)}, bf16[256,1024]{1,0:T(8,128)(2,1)S(1)}, u32[]{:S(2)}, u32[]{:S(2)}) %collective-permute-start) | collective-permute-done | bytes 524320 | tf_op jit(solution)/shard_map/keys_values/gather_1/z/ppermute | solution.py:45
  47.8 3.7 %collective-permute-start.2 = (bf16[256,1024]{1,0:T(8,128)(2,1)S(1)}, bf16[256,1024]{1,0:T(8,128)(2,1)S(1)}, u32[]{:S(2)}, u32[]{:S(2)}) collective-permute-start(bf16[256,1024]{1,0:T(8,128)(2,1)S(1)} %collective-permute-done.refs_1_), channel_id=1, source_target_pairs={{8,0},{12,4},{16,8},{20,12},{24,16},{28,20},{32,24},{36,28},{40,32... | collective-permute-start | bytes 1572872 | tf_op jit(solution)/shard_map/keys_values/gather_2/z/ppermute | solution.py:45
  51.5 8.3 %collective-permute-done.2.refs_3_ = bf16[256,1024]{1,0:T(8,128)(2,1)S(1)} collective-permute-done((bf16[256,1024]{1,0:T(8,128)(2,1)S(1)}, bf16[256,1024]{1,0:T(8,128)(2,1)S(1)}, u32[]{:S(2)}, u32[]{:S(2)}) %collective-permute-start.2) | collective-permute-done | bytes 524320 | tf_op jit(solution)/shard_map/keys_values/gather_2/z/ppermute | solution.py:45
  59.7 3.7 %collective-permute-start.4 = (bf16[256,1024]{1,0:T(8,128)(2,1)S(1)}, bf16[256,1024]{1,0:T(8,128)(2,1)S(1)}, u32[]{:S(2)}, u32[]{:S(2)}) collective-permute-start(bf16[256,1024]{1,0:T(8,128)(2,1)S(1)} %collective-permute-done.2.refs_3_), channel_id=1, source_target_pairs={{8,0},{12,4},{16,8},{20,12},{24,16},{28,20},{32,24},{36,28},{40,32... | collective-permute-start | bytes 1572872 | tf_op jit(solution)/shard_map/keys_values/gather_3/z/ppermute | solution.py:45
  63.5 7.6 %collective-permute-done.4.refs_5_ = bf16[256,1024]{1,0:T(8,128)(2,1)S(1)} collective-permute-done((bf16[256,1024]{1,0:T(8,128)(2,1)S(1)}, bf16[256,1024]{1,0:T(8,128)(2,1)S(1)}, u32[]{:S(2)}, u32[]{:S(2)}) %collective-permute-start.4) | collective-permute-done | bytes 524320 | tf_op jit(solution)/shard_map/keys_values/gather_3/z/ppermute | solution.py:45
  71.8 3.7 %collective-permute-start.6 = (bf16[128,1024]{1,0:T(8,128)(2,1)}, bf16[128,1024]{1,0:T(8,128)(2,1)S(1)}, u32[]{:S(2)}, u32[]{:S(2)}) collective-permute-start(bf16[128,1024]{1,0:T(8,128)(2,1)} %slice.95), channel_id=1, source_target_pairs={{8,0},{12,4},{16,8},{20,12},{24,16},{28,20},{32,24},{36,28},{40,32... | collective-permute-start | bytes 786440 | tf_op jit(solution)/shard_map/keys_values/gather_far/z/ppermute | solution.py:45
  77.2 8.6 %all-gather.5.cloned.1.call-done = bf16[12416,512]{1,0:T(8,128)(2,1)} async-done(((bf16[1552,512]{1,0:T(8,128)(2,1)}), bf16[12416,512]{1,0:T(8,128)(2,1)}) %all-gather.5.cloned.1.call-update) | async-done | bytes 12714000 | tf_op jit(solution)/shard_map/spans/all_gather | solution.py:294
  87.9 16.7 %attend.2 = (bf16[8,768,512]{2,1,0:T(8,128)(2,1)}, f32[8,512,256]{2,1,0:T(8,128)}) custom-call(s32[1]{0:T(128)} %bitcast.3.number, s32[96]{0:T(128)S(1)} %get-tuple-element.35.listed, s32[96]{0:T(128)S(1)} %get-tuple-element.34.block, s32[192]{0:T(256)S(1)} %reshape.241.ids, bf16[8,1552,512]{2,1,0:T(8,128)(2,1)} %bitcast.45, ...), custom_call_target="tpu_custom_call" | custom-call | flops 1610612736 | bytes 29360128 | tf_op jit(solution)/shard_map/attend/pallas_call | solution.py:221
  104.7 3.8 %dynamic-slice_bitcast_fusion.1 = bf16[4,768,512]{2,1,0:T(8,128)(2,1)} fusion(bf16[4,2,768,512]{3,2,1,0:T(8,128)(2,1)} %bitcast.49, s32[]{:T(128)S(6)} %select_n.178), kind=kLoop, calls=%fused_computation.3 | loop fusion | bytes 6291460 | tf_op jit(solution)/shard_map/attended/jit(dynamic_index_in_dim)/squeeze | solution.py:323
  108.6 5.8 %collective-permute-done.8 = bf16[4,768,512]{2,1,0:T(8,128)(2,1)} collective-permute-done((bf16[4,768,512]{2,1,0:T(8,128)(2,1)}, bf16[4,768,512]{2,1,0:T(8,128)(2,1)}, u32[]{:S(2)}, u32[]{:S(2)}) %collective-permute-start.8) | collective-permute-done | bytes 3145760 | tf_op jit(solution)/shard_map/attended/swap/ppermute | solution.py:35
  114.4 5.1 %bitcast_add_fusion.1 = bf16[4,768,512]{2,1,0:T(8,128)(2,1)} fusion(bf16[4,768,512]{2,1,0:T(8,128)(2,1)} %collective-permute-done.8, bf16[4,2,768,512]{3,2,1,0:T(8,128)(2,1)} %bitcast.50, s32[]{:T(128)S(6)} %select_n.177), kind=kLoop, calls=%fused_computation.1 | loop fusion | flops 1572864 | bytes 9437188 | tf_op jit(solution)/shard_map/attended/add | solution.py:325
  119.6 38.9 %all-gather.7.cloned.1.call-done = bf16[12416,512]{1,0:T(8,128)(2,1)} async-done(((bf16[1552,512]{1,0:T(8,128)(2,1)}), bf16[12416,512]{1,0:T(8,128)(2,1)}) %all-gather.7.cloned.1.call-update) | async-done | bytes 12714000 | tf_op jit(solution)/shard_map/spans/all_gather | solution.py:294
  160.6 16.2 %attend.3 = (bf16[8,768,512]{2,1,0:T(8,128)(2,1)}, bf16[512,256]{1,0:T(8,128)(2,1)S(1)}, bf16[512,256]{1,0:T(8,128)(2,1)S(1)}, bf16[512,256]{1,0:T(8,128)(2,1)S(...) custom-call(s32[1]{0:T(128)} %bitcast.12.number, ...), custom_call_target="tpu_custom_call" | custom-call | flops 1610612736 | bytes 29360128 | tf_op jit(solution)/shard_map/attend/pallas_call | solution.py:221
  179.1 5.6 %collective-permute-done.9 = bf16[4,768,512]{2,1,0:T(8,128)(2,1)S(1)} collective-permute-done((bf16[4,768,512]{2,1,0:T(8,128)(2,1)S(1)}, bf16[4,768,512]{2,1,0:T(8,128)(2,1)S(1)}, u32[]{:S(2)}, u32[]{:S(2)}) %collective-permute-start.9) | collective-permute-done | bytes 3145760 | tf_op jit(solution)/shard_map/attended/swap/ppermute | solution.py:35
  186.9 4.3 %collective-permute-start.15 = (bf16[256,256]{1,0:T(8,128)(2,1)S(1)}, bf16[256,256]{1,0:T(8,128)(2,1)S(1)}, u32[]{:S(2)}, u32[]{:S(2)}) collective-permute-start(bf16[256,256]{1,0:T(8,128)(2,1)S(1)} %get-tuple-element.27), channel_id=1, source_target_pairs={{8,0},{12,4},{16,8},{20,12},{24,16},{28,20},{32,24},{36,28},{40,32... | collective-permute-start | bytes 393224 | tf_op jit(solution)/shard_map/key_gradients/scatter_far/z/ppermute | solution.py:45
  191.2 3.7 %collective-permute-done.11 = bf16[256,256]{1,0:T(8,128)(2,1)S(1)} collective-permute-done((bf16[256,256]{1,0:T(8,128)(2,1)S(1)}, bf16[256,256]{1,0:T(8,128)(2,1)S(1)}, u32[]{:S(2)}, u32[]{:S(2)}) %collective-permute-start.11) | collective-permute-done | bytes 131104 | tf_op jit(solution)/shard_map/key_gradients/scatter_far/z/ppermute | solution.py:45
  198.4 5.8 %collective-permute-done.12 = bf16[512,256]{1,0:T(8,128)(2,1)S(1)} collective-permute-done((bf16[512,256]{1,0:T(8,128)(2,1)S(1)}, bf16[512,256]{1,0:T(8,128)(2,1)S(1)}, u32[]{:S(2)}, u32[]{:S(2)}) %collective-permute-start.12) | collective-permute-done | bytes 262176 | tf_op jit(solution)/shard_map/key_gradients/scatter_3/z/ppermute | solution.py:45
  207.7 4.9 %collective-permute-done.13 = bf16[512,256]{1,0:T(8,128)(2,1)S(1)} collective-permute-done((bf16[512,256]{1,0:T(8,128)(2,1)S(1)}, bf16[512,256]{1,0:T(8,128)(2,1)S(1)}, u32[]{:S(2)}, u32[]{:S(2)}) %collective-permute-start.13) | collective-permute-done | bytes 262176 | tf_op jit(solution)/shard_map/key_gradients/scatter_2/z/ppermute | solution.py:45
  212.8 3.3 %collective-permute-start.18 = (bf16[512,256]{1,0:T(8,128)(2,1)S(1)}, bf16[512,256]{1,0:T(8,128)(2,1)S(1)}, u32[]{:S(2)}, u32[]{:S(2)}) collective-permute-start(bf16[512,256]{1,0:T(8,128)(2,1)S(1)} %add_convert_fusion.1), channel_id=1, source_target_pairs={{8,0},{12,4},{16,8},{20,12},{24,16},{28,20},{32,24},{36,28},{40,32... | collective-permute-start | bytes 786440 | tf_op jit(solution)/shard_map/key_gradients/scatter_1/z/ppermute | solution.py:45
  216.3 4.0 %collective-permute-done.14 = bf16[512,256]{1,0:T(8,128)(2,1)S(1)} collective-permute-done((bf16[512,256]{1,0:T(8,128)(2,1)S(1)}, bf16[512,256]{1,0:T(8,128)(2,1)S(1)}, u32[]{:S(2)}, u32[]{:S(2)}) %collective-permute-start.14) | collective-permute-done | bytes 262176 | tf_op jit(solution)/shard_map/key_gradients/scatter_1/z/ppermute | solution.py:45
  222.7 29.5 %all_to_all.10 = bf16[4,8,24,512]{3,2,1,0:T(8,128)(2,1)S(1)} all-to-all(bf16[4,8,24,512]{3,2,1,0:T(8,128)(2,1)S(1)} %bitcast.52), channel_id=1, replica_groups={{0,64,128,192},{4,68,132,196},{8,72,136,200},{12,76,140,204},{16,80,144..., dimensions={0} | all-to-all | bytes 1572864 | tf_op jit(solution)/shard_map/all_to_all | solution.py:273
  252.3 14.5 %all_to_all.11 = bf16[8,1,24,512]{3,2,1,0:T(8,128)(2,1)S(1)} all-to-all(bf16[8,1,24,512]{3,2,1,0:T(8,128)(2,1)S(1)} %bitcast.51), channel_id=1, replica_groups={{0,8,16,24,32,40,48,56},{4,12,20,28,36,44,52,60},{64,72,80,88,96,104,11..., dimensions={0} | all-to-all | bytes 393216 | tf_op jit(solution)/shard_map/all_to_all | solution.py:273
  (126 shorter events, 34.7 us)
Async XLA Ops:
  7.2 78.6 %all-gather.5.cloned.1.call-start = ((), (), s32[]{:S(2)}) async-start(), calls=%async_computation.6 | async-start | bytes 14303232 | tf_op jit(solution)/shard_map/spans/all_gather | solution.py:294
  12.2 146.3 %all-gather.7.cloned.1.call-start = ((), (), s32[]{:S(2)}) async-start(), calls=%async_computation.7 | async-start | bytes 14303232 | tf_op jit(solution)/shard_map/spans/all_gather | solution.py:294
  13.6 253.8 %reduce-scatter.3.cloned.1.call-start = ((), (), s32[]{:S(2)}) async-start(), calls=%async_computation.4 | async-start | bytes 3932160 | tf_op jit(solution)/shard_map/attended/reduce_scatter | solution.py:327
  33.8 13.9 %collective-permute-start = (bf16[256,1024]{1,0:T(8,128)(2,1)S(1)}, bf16[256,1024]{1,0:T(8,128)(2,1)S(1)}, u32[]{:S(2)}, u32[]{:S(2)}) collective-permute-start(bf16[256,1024]{1,0:T(8,128)(2,1)S(1)} %pad_maximum_fusion.3.refs_0_), channel_id=1, source_target_pairs={{8,0},{12,4},{16,8},{20,12},{24,16},{28,20},{32,24},{36,28},{40,32... | collective-permute-start | bytes 1572872 | tf_op jit(solution)/shard_map/keys_values/gather_1/z/ppermute | solution.py:45
  39.5 12.0 %collective-permute-start.1 = (bf16[256,1024]{1,0:T(8,128)(2,1)S(1)}, bf16[256,1024]{1,0:T(8,128)(2,1)S(1)}, u32[]{:S(2)}, u32[]{:S(2)}) collective-permute-start(bf16[256,1024]{1,0:T(8,128)(2,1)S(1)} %pad_maximum_fusion.3.refs_0_), channel_id=1, source_target_pairs={{56,0},{60,4},{0,8},{4,12},{8,16},{12,20},{16,24},{20,28},{24,32},... | collective-permute-start | bytes 1572872 | tf_op jit(solution)/shard_map/keys_values/gather_1/z/ppermute | solution.py:45
  47.8 12.0 %collective-permute-start.2 = (bf16[256,1024]{1,0:T(8,128)(2,1)S(1)}, bf16[256,1024]{1,0:T(8,128)(2,1)S(1)}, u32[]{:S(2)}, u32[]{:S(2)}) collective-permute-start(bf16[256,1024]{1,0:T(8,128)(2,1)S(1)} %collective-permute-done.refs_1_), channel_id=1, source_target_pairs={{8,0},{12,4},{16,8},{20,12},{24,16},{28,20},{32,24},{36,28},{40,32... | collective-permute-start | bytes 1572872 | tf_op jit(solution)/shard_map/keys_values/gather_2/z/ppermute | solution.py:45
  51.4 12.0 %collective-permute-start.3 = (bf16[256,1024]{1,0:T(8,128)(2,1)S(1)}, bf16[256,1024]{1,0:T(8,128)(2,1)S(1)}, u32[]{:S(2)}, u32[]{:S(2)}) collective-permute-start(bf16[256,1024]{1,0:T(8,128)(2,1)S(1)} %collective-permute-done.1.refs_2_), channel_id=1, source_target_pairs={{56,0},{60,4},{0,8},{4,12},{8,16},{12,20},{16,24},{20,28},{24,32},... | collective-permute-start | bytes 1572872 | tf_op jit(solution)/shard_map/keys_values/gather_2/z/ppermute | solution.py:45
  59.7 11.3 %collective-permute-start.4 = (bf16[256,1024]{1,0:T(8,128)(2,1)S(1)}, bf16[256,1024]{1,0:T(8,128)(2,1)S(1)}, u32[]{:S(2)}, u32[]{:S(2)}) collective-permute-start(bf16[256,1024]{1,0:T(8,128)(2,1)S(1)} %collective-permute-done.2.refs_3_), channel_id=1, source_target_pairs={{8,0},{12,4},{16,8},{20,12},{24,16},{28,20},{32,24},{36,28},{40,32... | collective-permute-start | bytes 1572872 | tf_op jit(solution)/shard_map/keys_values/gather_3/z/ppermute | solution.py:45
  63.4 12.1 %collective-permute-start.5 = (bf16[256,1024]{1,0:T(8,128)(2,1)S(1)}, bf16[256,1024]{1,0:T(8,128)(2,1)}, u32[]{:S(2)}, u32[]{:S(2)}) collective-permute-start(bf16[256,1024]{1,0:T(8,128)(2,1)S(1)} %collective-permute-done.3.refs_4_), channel_id=1, source_target_pairs={{56,0},{60,4},{0,8},{4,12},{8,16},{12,20},{16,24},{20,28},{24,32},... | collective-permute-start | bytes 1572872 | tf_op jit(solution)/shard_map/keys_values/gather_3/z/ppermute | solution.py:45
  71.8 16.1 %collective-permute-start.6 = (bf16[128,1024]{1,0:T(8,128)(2,1)}, bf16[128,1024]{1,0:T(8,128)(2,1)S(1)}, u32[]{:S(2)}, u32[]{:S(2)}) collective-permute-start(bf16[128,1024]{1,0:T(8,128)(2,1)} %slice.95), channel_id=1, source_target_pairs={{8,0},{12,4},{16,8},{20,12},{24,16},{28,20},{32,24},{36,28},{40,32... | collective-permute-start | bytes 786440 | tf_op jit(solution)/shard_map/keys_values/gather_far/z/ppermute | solution.py:45
  77.2 10.7 %collective-permute-start.7 = (bf16[128,1024]{1,0:T(8,128)(2,1)}, bf16[128,1024]{1,0:T(8,128)(2,1)}, u32[]{:S(2)}, u32[]{:S(2)}) collective-permute-start(bf16[128,1024]{1,0:T(8,128)(2,1)} %slice.96), channel_id=1, source_target_pairs={{56,0},{60,4},{0,8},{4,12},{8,16},{12,20},{16,24},{20,28},{24,32},... | collective-permute-start | bytes 786440 | tf_op jit(solution)/shard_map/keys_values/gather_far/z/ppermute | solution.py:45
  108.4 6.0 %collective-permute-start.8 = (bf16[4,768,512]{2,1,0:T(8,128)(2,1)}, bf16[4,768,512]{2,1,0:T(8,128)(2,1)}, u32[]{:S(2)}, u32[]{:S(2)}) collective-permute-start(bf16[4,768,512]{2,1,0:T(8,128)(2,1)} %dynamic-slice_bitcast_fusion.1), channel_id=1, source_target_pairs={{0,4},{4,0},{8,12},{12,8},{16,20},{20,16},{24,28},{28,24},{32,36},... | collective-permute-start | bytes 9437192 | tf_op jit(solution)/shard_map/attended/swap/ppermute | solution.py:35
  119.5 148.0 %reduce-scatter.5.cloned.1.call-start = ((), (), s32[]{:S(2)}) async-start(), calls=%async_computation.5 | async-start | bytes 3932160 | tf_op jit(solution)/shard_map/attended/reduce_scatter | solution.py:327
  179.0 5.7 %collective-permute-start.9 = (bf16[4,768,512]{2,1,0:T(8,128)(2,1)S(1)}, bf16[4,768,512]{2,1,0:T(8,128)(2,1)S(1)}, u32[]{:S(2)}, u32[]{:S(2)}) collective-permute-start(bf16[4,768,512]{2,1,0:T(8,128)(2,1)S(1)} %dynamic-slice_bitcast_fusion), channel_id=1, source_target_pairs={{0,4},{4,0},{8,12},{12,8},{16,20},{20,16},{24,28},{28,24},{32,36},... | collective-permute-start | bytes 9437192 | tf_op jit(solution)/shard_map/attended/swap/ppermute | solution.py:35
  186.8 8.1 %collective-permute-start.11 = (bf16[256,256]{1,0:T(8,128)(2,1)S(1)}, bf16[256,256]{1,0:T(8,128)(2,1)S(1)}, u32[]{:S(2)}, u32[]{:S(2)}) collective-permute-start(bf16[256,256]{1,0:T(8,128)(2,1)S(1)} %get-tuple-element.23), channel_id=1, source_target_pairs={{56,0},{60,4},{0,8},{4,12},{8,16},{12,20},{16,24},{20,28},{24,32},... | collective-permute-start | bytes 393224 | tf_op jit(solution)/shard_map/key_gradients/scatter_far/z/ppermute | solution.py:45
  186.9 8.2 %collective-permute-start.15 = (bf16[256,256]{1,0:T(8,128)(2,1)S(1)}, bf16[256,256]{1,0:T(8,128)(2,1)S(1)}, u32[]{:S(2)}, u32[]{:S(2)}) collective-permute-start(bf16[256,256]{1,0:T(8,128)(2,1)S(1)} %get-tuple-element.27), channel_id=1, source_target_pairs={{8,0},{12,4},{16,8},{20,12},{24,16},{28,20},{32,24},{36,28},{40,32... | collective-permute-start | bytes 393224 | tf_op jit(solution)/shard_map/key_gradients/scatter_far/z/ppermute | solution.py:45
  194.9 9.2 %collective-permute-start.12 = (bf16[512,256]{1,0:T(8,128)(2,1)S(1)}, bf16[512,256]{1,0:T(8,128)(2,1)S(1)}, u32[]{:S(2)}, u32[]{:S(2)}) collective-permute-start(bf16[512,256]{1,0:T(8,128)(2,1)S(1)} %pad_maximum_fusion.4), channel_id=1, source_target_pairs={{56,0},{60,4},{0,8},{4,12},{8,16},{12,20},{16,24},{20,28},{24,32},... | collective-permute-start | bytes 786440 | tf_op jit(solution)/shard_map/key_gradients/scatter_3/z/ppermute | solution.py:45
  195.1 9.2 %collective-permute-start.16 = (bf16[512,256]{1,0:T(8,128)(2,1)S(1)}, bf16[512,256]{1,0:T(8,128)(2,1)S(1)}, u32[]{:S(2)}, u32[]{:S(2)}) collective-permute-start(bf16[512,256]{1,0:T(8,128)(2,1)S(1)} %pad_maximum_fusion.5), channel_id=1, source_target_pairs={{8,0},{12,4},{16,8},{20,12},{24,16},{28,20},{32,24},{36,28},{40,32... | collective-permute-start | bytes 786440 | tf_op jit(solution)/shard_map/key_gradients/scatter_3/z/ppermute | solution.py:45
  204.3 8.3 %collective-permute-start.13 = (bf16[512,256]{1,0:T(8,128)(2,1)S(1)}, bf16[512,256]{1,0:T(8,128)(2,1)S(1)}, u32[]{:S(2)}, u32[]{:S(2)}) collective-permute-start(bf16[512,256]{1,0:T(8,128)(2,1)S(1)} %add_convert_fusion.4), channel_id=1, source_target_pairs={{56,0},{60,4},{0,8},{4,12},{8,16},{12,20},{16,24},{20,28},{24,32},... | collective-permute-start | bytes 786440 | tf_op jit(solution)/shard_map/key_gradients/scatter_2/z/ppermute | solution.py:45
  204.4 8.3 %collective-permute-start.17 = (bf16[512,256]{1,0:T(8,128)(2,1)S(1)}, bf16[512,256]{1,0:T(8,128)(2,1)S(1)}, u32[]{:S(2)}, u32[]{:S(2)}) collective-permute-start(bf16[512,256]{1,0:T(8,128)(2,1)S(1)} %add_convert_fusion.2), channel_id=1, source_target_pairs={{8,0},{12,4},{16,8},{20,12},{24,16},{28,20},{32,24},{36,28},{40,32... | collective-permute-start | bytes 786440 | tf_op jit(solution)/shard_map/key_gradients/scatter_2/z/ppermute | solution.py:45
  212.7 7.7 %collective-permute-start.14 = (bf16[512,256]{1,0:T(8,128)(2,1)S(1)}, bf16[512,256]{1,0:T(8,128)(2,1)S(1)}, u32[]{:S(2)}, u32[]{:S(2)}) collective-permute-start(bf16[512,256]{1,0:T(8,128)(2,1)S(1)} %add_convert_fusion.3), channel_id=1, source_target_pairs={{56,0},{60,4},{0,8},{4,12},{8,16},{12,20},{16,24},{20,28},{24,32},... | collective-permute-start | bytes 786440 | tf_op jit(solution)/shard_map/key_gradients/scatter_1/z/ppermute | solution.py:45
  212.8 7.5 %collective-permute-start.18 = (bf16[512,256]{1,0:T(8,128)(2,1)S(1)}, bf16[512,256]{1,0:T(8,128)(2,1)S(1)}, u32[]{:S(2)}, u32[]{:S(2)}) collective-permute-start(bf16[512,256]{1,0:T(8,128)(2,1)S(1)} %add_convert_fusion.1), channel_id=1, source_target_pairs={{8,0},{12,4},{16,8},{20,12},{24,16},{28,20},{32,24},{36,28},{40,32... | collective-permute-start | bytes 786440 | tf_op jit(solution)/shard_map/key_gradients/scatter_1/z/ppermute | solution.py:45
  216.2 4.3 %collective-permute-start.10 = (bf16[256,32,24]{0,2,1:T(8,128)(2,1)S(1)}, bf16[256,32,24]{0,2,1:T(8,128)(2,1)S(1)}, u32[]{:S(2)}, u32[]{:S(2)}) collective-permute-start(bf16[256,32,24]{0,2,1:T(8,128)(2,1)S(1)} %get-tuple-element.41), channel_id=1, source_target_pairs={{0,4},{4,0},{8,12},{12,8},{16,20},{20,16},{24,28},{28,24},{32,36},... | collective-permute-start | bytes 1179656 | tf_op jit(solution)/shard_map/swap/ppermute | solution.py:35
  220.4 1.6 collective-permute-start.19
  (12 other events, 281.0 us)
Sparse Core Ops, SparseCore 0:
  12.3 73.4 all-gather.4
  87.6 70.8 all-gather.6
  161.1 41.2 reduce-scatter.2
  204.8 48.9 reduce-scatter.4
